TPU v7x, 128 devices: a whole 4x4x4 slice. The times are simulated.
128 devices in a mesh: dp: 8 (over z, core), tp: 16 (over y, x).
Axes of the slice: x: 4, y: 4, z: 4, core: 2. Of those that a mesh axis runs over, the one named last changes fastest.
Arguments:
- tokens: bfloat16 [8192, 3584], P('dp', 'tp'), may hold values from -6 to 6
- routes: int32 [8192, 8], P('dp'), may hold values from 0 to 127, all different within a row; in each aligned block of 1024 rows (0 to 1023, 1024 to 2047, ...) at most 66 rows name the same one
- route_weights: float32 [8192, 8], P('dp'), may hold values from 0.1 to 0.6
- expert_owner: int32 [128], replicated, may hold values from 0 to 127, each once
- expert_gate_up: bfloat16 [128, 3584, 2048], P(('dp', 'tp')), may hold values from -0.09375 to 0.09375
- expert_down: bfloat16 [128, 1024, 3584], P(('dp', 'tp')), may hold values from -0.1875 to 0.1875
- shared_gate_up: bfloat16 [3584, 2, 2048], P(None, None, 'tp'), may hold values from -0.09375 to 0.09375
- shared_down: bfloat16 [2048, 3584], P(None, 'tp'), may hold values from -0.125 to 0.125
Outputs:
- moe_output: bfloat16 [8192, 3584], P('dp', 'tp')
Inputs may be any that keep to these rules, and one draw needn't show every extreme that they name: `routes`: in each aligned block of 1024 rows (the rows of one index of dp) no expert is named by more than 66 rows, a bound that some block reaches; each row names 8 different experts. A permutation: the device at position s of the mesh, dp-major, holds expert expert_owner[s].
All inputs are finite; a program needn't handle non-finite values.
Results may differ from a plain program's by a relative error of at most 0.0095.
Values may be sent and summed in bfloat16 or wider, within the bound.
No kernel may reach another device: no remote copies, remote signals or barrier semaphores. Data moves between devices by JAX's collectives and lax.ppermute only.
A program may use at most 192 MiB of HBM per device.

v0:
```python
import functools

import jax
import jax.numpy as jnp
from jax import lax
from jax.experimental import pallas as pl
from jax.experimental.pallas import tpu as pltpu
from jax.sharding import PartitionSpec as P

F32 = jnp.float32
BF16 = jnp.bfloat16
SIDE = 4
ROW = 72
PACK = 120
VMEM = 40 * 1024 * 1024


def params(semantics=None, vmem=VMEM):
    return pltpu.CompilerParams(vmem_limit_bytes=vmem, dimension_semantics=semantics)


def whole(space=pltpu.VMEM):
    return pl.BlockSpec(memory_space=space)


def dot(a, b, dims):
    return lax.dot_general(a, b, (dims, ((), ())), preferred_element_type=F32)


def pack(low, high):
    lane = lax.broadcasted_iota(jnp.int32, (48, 128), 1)
    line = lax.broadcasted_iota(jnp.int32, (8, 128), 0)
    tail = high[48:64]
    moved = jnp.concatenate([pltpu.roll(tail, 96 - 32 * q, 1) for q in range(3)], axis=0)
    second = jnp.where(lane < 96, high[:48], moved)
    extra = jnp.where(line < 2, low[64:72], pltpu.roll(high[64:72], 2, 0))
    return jnp.concatenate([low[:64], second, extra], axis=0).astype(BF16)


def unpack_tail(second):
    lane = lax.broadcasted_iota(jnp.int32, (16, 128), 1)
    tail = jnp.zeros((16, 128), F32)
    for q in range(3):
        moved = pltpu.roll(second[16 * q : 16 * q + 16], 32 + 32 * q, 1)
        tail = jnp.where((lane >= 32 * q) & (lane < 32 * q + 32), moved, tail)
    return tail


def unpack(block):
    block = block.astype(F32)
    line = lax.broadcasted_iota(jnp.int32, (8, 128), 0)
    second, extra = block[64:112], block[112:120]
    low = jnp.concatenate([block[:64], jnp.where(line < 2, extra, 0.0)], axis=0)
    last = jnp.where(line < 2, pltpu.roll(extra, 6, 0), 0.0)
    high = jnp.concatenate([second, unpack_tail(second), last], axis=0)
    return jnp.concatenate([low, high[:, :96]], axis=1)


def dispatch_kernel(per_step, routes_ref, weights_ref, owner_ref, tokens_ref, rank_ref, weight_ref, out_ref):
    experts, tokens = rank_ref.shape
    feats = tokens_ref.shape[0]
    step = pl.program_id(0)

    @pl.when(step == 0)
    def _():
        owner = jnp.broadcast_to(owner_ref[...], (experts, experts)).astype(F32).T[:, :1]
        routes = routes_ref[...].astype(F32)
        hit = jnp.zeros((experts, tokens), F32)
        weight = jnp.zeros((experts, tokens), F32)
        for k in range(routes_ref.shape[0]):
            same = owner == routes[k : k + 1, :]
            hit = jnp.where(same, 1.0, hit)
            weight = jnp.where(same, weights_ref[k : k + 1, :], weight)
        weight_ref[...] = weight
        earlier = lax.broadcasted_iota(jnp.int32, (tokens, tokens), 0)
        later = lax.broadcasted_iota(jnp.int32, (tokens, tokens), 1)
        before = jnp.where(earlier < later, 1.0, 0.0).astype(BF16)
        rank = dot(hit.astype(BF16), before, ((1,), (0,)))
        rank_ref[...] = jnp.where(hit > 0.0, rank, -1.0)

    place = lax.broadcasted_iota(jnp.int32, (ROW, tokens), 0).astype(F32)
    rank = rank_ref[pl.ds(pl.multiple_of(step * per_step, per_step), per_step), :]
    pick = [jnp.where(place == rank[e : e + 1, :], 1.0, 0.0) for e in range(per_step)]
    pick = jnp.concatenate(pick, axis=0).astype(BF16)
    feat = jnp.concatenate([tokens_ref[...], jnp.zeros((256 - feats, tokens), BF16)], axis=0)
    res = dot(pick, feat, ((1,), (1,)))
    for e in range(per_step):
        rows = res[e * ROW : (e + 1) * ROW]
        out_ref[e] = pack(rows[:, :128], rows[:, 128:])


def dispatch(routes, weights, owner, tokens, per_step=16):
    experts, count = owner.shape[1], routes.shape[1]
    fixed = lambda a: pl.BlockSpec(a.shape, lambda i: (0, 0))
    table = jax.ShapeDtypeStruct((experts, count), F32)
    return pl.pallas_call(
        functools.partial(dispatch_kernel, per_step),
        out_shape=(table, table, jax.ShapeDtypeStruct((experts, PACK, 128), BF16)),
        grid=(experts // per_step,),
        in_specs=[fixed(routes), fixed(weights), fixed(owner), fixed(tokens)],
        out_specs=(
            fixed(table),
            fixed(table),
            pl.BlockSpec((per_step, PACK, 128), lambda i: (i, 0, 0)),
        ),
        compiler_params=params(("arbitrary",), 60 * 1024 * 1024),
        cost_estimate=pl.CostEstimate(
            flops=2 * experts * ROW * 256 * count, bytes_accessed=6 * 10**6, transcendentals=0
        ),
    )(routes, weights, owner, tokens)


def expert_kernel(tile, got_in, up_in, down_in, out_ref, got, up_w, down_w, x, act, held, sems):
    groups, n_tensor = out_ref.shape[:2]
    share = n_tensor // SIDE
    hidden = act.shape[1]
    wide = x.shape[1] // SIDE
    feats = wide // share
    tiles = hidden // tile

    def got_copy(k):
        return pltpu.make_async_copy(
            got_in.at[:, pl.ds(k * share, share)], got.at[k], sems.at[k]
        )

    def up_copy(n):
        cols = pl.ds(n * tile, tile)
        return pltpu.make_async_copy(up_in.at[:, cols], up_w.at[:, cols], sems.at[SIDE + n])

    def down_copy(y):
        cols = pl.ds(y * wide, wide)
        at = SIDE + 2 * tiles + y
        return pltpu.make_async_copy(down_in.at[:, cols], down_w.at[:, cols], sems.at[at])

    def out_copy(y):
        at = 2 * SIDE + 2 * tiles + y
        return pltpu.make_async_copy(
            held.at[y], out_ref.at[:, pl.ds(y * share, share)], sems.at[at]
        )

    for k in range(SIDE):
        got_copy(k).start()
    for n in range(tiles):
        up_copy(n).start()
        up_copy(tiles + n).start()
    for y in range(SIDE):
        down_copy(y).start()

    for k in range(SIDE):
        got_copy(k).wait()
        for d in range(0, groups, 2):
            rows = []
            for i in (d, d + 1):
                parts = [unpack(got[k, i, t]) for t in range(share)]
                rows.append(jnp.concatenate(parts, axis=1))
            x[d * ROW : (d + 2) * ROW, k * wide : (k + 1) * wide] = jnp.concatenate(
                rows, axis=0
            ).astype(BF16)

    for n in range(tiles):
        up_copy(n).wait()
        up_copy(tiles + n).wait()
        low = slice(n * tile, (n + 1) * tile)
        high = slice(hidden + n * tile, hidden + (n + 1) * tile)
        gate = dot(x[...], up_w[:, low], ((1,), (0,)))
        up = dot(x[...], up_w[:, high], ((1,), (0,)))
        act[:, low] = (gate / (1.0 + jnp.exp(-gate)) * up).astype(BF16)

    for y in range(SIDE):
        down_copy(y).wait()
        res = dot(act[...], down_w[:, y * wide : (y + 1) * wide], ((1,), (0,)))
        for t in range(share):
            low = res[:, t * feats : t * feats + 128]
            high = res[:, t * feats + 128 : (t + 1) * feats]
            blank = jnp.zeros((res.shape[0], 256 - feats), F32)
            high = jnp.concatenate([high, blank], axis=1)
            for d in range(groups):
                block = slice(d * ROW, (d + 1) * ROW)
                held[y, d, t] = pack(low[block], high[block])
        out_copy(y).start()
    for y in range(SIDE):
        out_copy(y).wait()


def expert(got, up_weights, down_weights, tile=256):
    groups, n_tensor = got.shape[:2]
    rows = groups * ROW
    width, both = up_weights.shape
    hidden = both // 2
    blocks = pltpu.VMEM((SIDE, groups, n_tensor // SIDE, PACK, 128), BF16)
    return pl.pallas_call(
        functools.partial(expert_kernel, tile),
        out_shape=jax.ShapeDtypeStruct(got.shape, BF16),
        in_specs=[whole(pl.ANY)] * 3,
        out_specs=whole(pl.ANY),
        scratch_shapes=[
            blocks,
            pltpu.VMEM((width, both), BF16),
            pltpu.VMEM((hidden, width), BF16),
            pltpu.VMEM((rows, width), BF16),
            pltpu.VMEM((rows, hidden), BF16),
            blocks,
            pltpu.SemaphoreType.DMA((3 * SIDE + both // tile,)),
        ],
        compiler_params=params(vmem=60 * 1024 * 1024),
        cost_estimate=pl.CostEstimate(
            flops=6 * rows * width * hidden, bytes_accessed=6 * width * hidden, transcendentals=0
        ),
    )(got, up_weights, down_weights)


def spread_kernel(rank_ref, weight_ref, main_ref, late_ref):
    experts, tokens = rank_ref.shape
    place = lax.broadcasted_iota(jnp.int32, (64, tokens), 0).astype(F32)
    line = lax.broadcasted_iota(jnp.int32, (8, tokens), 0)
    late = jnp.where(line < 4, jnp.where(line % 2 == 0, 64.0, 65.0), -2.0)
    extra = []
    for e in range(0, experts, 2):
        pair = []
        for i in (e, e + 1):
            rank = rank_ref[i : i + 1, :]
            weight = weight_ref[i : i + 1, :]
            pair.append(jnp.where(place == rank, weight, 0.0))
            extra.append(jnp.where(late == rank, weight, 0.0))
        main_ref[:, e * 64 : (e + 2) * 64] = jnp.concatenate(pair, axis=0).astype(BF16).T
    late_ref[...] = jnp.concatenate(extra, axis=0).astype(BF16).T


def spread(rank, weight, per_step=16):
    experts, tokens = rank.shape
    lines = pl.BlockSpec((per_step, tokens), lambda i: (i, 0))
    block = lambda rows: pl.BlockSpec((tokens, per_step * rows), lambda i: (0, i))
    return pl.pallas_call(
        spread_kernel,
        out_shape=(
            jax.ShapeDtypeStruct((tokens, experts * 64), BF16),
            jax.ShapeDtypeStruct((tokens, experts * 8), BF16),
        ),
        grid=(experts // per_step,),
        in_specs=[lines, lines],
        out_specs=(block(64), block(8)),
        compiler_params=params(("arbitrary",), 60 * 1024 * 1024),
        cost_estimate=pl.CostEstimate(
            flops=2 * experts * 64 * tokens, bytes_accessed=20 * 10**6, transcendentals=0
        ),
    )(rank, weight)


def combine_kernel(steps, back_ref, main_ref, late_ref, shared_ref, out_ref, total):
    step = pl.program_id(0)
    line = lax.broadcasted_iota(jnp.int32, (8, 128), 0)
    left, right, extra_l, extra_r = [], [], [], []
    for e in range(back_ref.shape[0]):
        left.append(back_ref[e, 0:64, :])
        second = back_ref[e, 64:112, :]
        tail = unpack_tail(second.astype(F32)).astype(BF16)
        right.append(jnp.concatenate([second, tail], axis=0))
        extra = back_ref[e, 112:120, :].astype(F32)
        extra_l.append(jnp.where(line < 2, extra, 0.0))
        extra_r.append(jnp.where((line >= 2) & (line < 4), extra, 0.0))
    rows = jnp.concatenate([jnp.concatenate(left, axis=0), jnp.concatenate(right, axis=0)], axis=1)
    late_rows = jnp.concatenate(
        [jnp.concatenate(extra_l, axis=0), jnp.concatenate(extra_r, axis=0)], axis=1
    ).astype(BF16)
    part = dot(main_ref[...], rows, ((1,), (0,))) + dot(late_ref[...], late_rows, ((1,), (0,)))

    @pl.when(step == 0)
    def _():
        total[...] = part

    @pl.when((step > 0) & (step < steps - 1))
    def _():
        total[...] += part

    @pl.when(step == steps - 1)
    def _():
        feats = out_ref.shape[0]
        out_ref[...] = ((total[...] + part).T[:feats] + shared_ref[...]).astype(BF16)


def combine(back, main, late, shared, per_step=32):
    experts = back.shape[0]
    tokens = main.shape[0]
    feats = shared.shape[0]
    steps = experts // per_step
    return pl.pallas_call(
        functools.partial(combine_kernel, steps),
        out_shape=jax.ShapeDtypeStruct((feats, tokens), BF16),
        grid=(steps,),
        in_specs=[
            pl.BlockSpec((per_step, PACK, 128), lambda i: (i, 0, 0)),
            pl.BlockSpec((tokens, per_step * 64), lambda i: (0, i)),
            pl.BlockSpec((tokens, per_step * 8), lambda i: (0, i)),
            pl.BlockSpec((feats, tokens), lambda i: (0, 0)),
        ],
        out_specs=pl.BlockSpec((feats, tokens), lambda i: (0, 0)),
        scratch_shapes=[pltpu.VMEM((tokens, 256), F32)],
        compiler_params=params(("arbitrary",), 56 * 1024 * 1024),
        cost_estimate=pl.CostEstimate(
            flops=2 * experts * 72 * 256 * tokens, bytes_accessed=24 * 10**6, transcendentals=0
        ),
    )(back, main, late, shared)


def on_device(
    tokens,
    routes,
    route_weights,
    expert_owner,
    expert_gate_up,
    expert_down,
    shared_gate_up,
    shared_down,
):
    groups = lax.axis_size("dp")
    n_tensor = lax.axis_size("tp")
    experts = groups * n_tensor
    features = tokens.T
    features_all = lax.all_gather(features, "tp", axis=0, tiled=True)
    rank, weight, blocks = dispatch(
        routes.T, route_weights.T, expert_owner.reshape(1, -1), features
    )

    def exchange(blocks):
        return lax.all_to_all(blocks, ("dp", "tp"), split_axis=0, concat_axis=0, tiled=True)

    got = exchange(blocks).reshape(groups, n_tensor, PACK, 128)
    packed = expert(got, expert_gate_up[0], expert_down[0])

    shared_gate_up, _ = lax.optimization_barrier((shared_gate_up, packed))
    shared_w = shared_gate_up.reshape(features_all.shape[0], -1)
    proj = dot(shared_w, features_all, ((0,), (0,)))
    units = proj.shape[0] // 2
    shared_act = (jax.nn.silu(proj[:units]) * proj[units:]).astype(BF16)
    shared_all = lax.all_gather(shared_act, "tp", axis=0, tiled=True)

    main, late = spread(rank, weight)
    back = exchange(packed.reshape(experts, PACK, 128))
    shared_out = dot(shared_down.T, shared_all, ((1,), (0,)))
    return combine(back, main, late, shared_out).T


def solution(mesh):
    return jax.shard_map(
        on_device,
        mesh=mesh,
        in_specs=(
            P("dp", "tp"),
            P("dp", None),
            P("dp", None),
            P(),
            P(("dp", "tp"), None, None),
            P(("dp", "tp"), None, None),
            P(None, None, "tp"),
            P(None, "tp"),
        ),
        out_specs=P("dp", "tp"),
        check_vma=False,
    )
```

profile of v0, /device:TPU:24, one launch (start us, length us, event | category | flops | bytes accessed | tf_op | source)
XLA Modules:
  0.0 228.5 jit_solution(5815522703897664191)
XLA Ops:
  6.5 0.0 copy-start
  6.5 0.0 all-gather.3.cloned.1.call-start
  6.5 0.7 all-gather.3.cloned.1.call-update
  7.3 0.0 all-gather.5.cloned.1.call-start
  7.3 9.8 %shard_map.82 = (f32[128,1024]{1,0:T(8,128)}, f32[128,1024]{1,0:T(8,128)}, bf16[128,120,128]{2,1,0:T(8,128)(2,1)}) custom-call(s32[8,1024]{1,0:T(8,128)} %bitcast.25, f32[8,1024]{1,0:T(8,128)} %bitcast.26, s32[1,128]{1,0:T(1,128)} %bitcast.27, bf16[224,1024]{1,0:T(8,128)(2,1)} %bitcast.22), custom_call_target="tpu_custom_call" | custom-call | flops 4831838208 | bytes 6000000 | tf_op jit(solution)/shard_map/pallas_call | solution.py:96
  17.1 63.1 %all_to_all.10 = bf16[128,120,128]{2,1,0:T(8,128)(2,1)} all-to-all(bf16[128,120,128]{2,1,0:T(8,128)(2,1)} %get-tuple-element.11), channel_id=1, replica_groups=mesh['dp'=8,'tp'=16] {'dp','tp'}, dimensions={0} | all-to-all | bytes 7864320 | tf_op jit(solution)/shard_map/all_to_all | solution.py:325
  80.2 0.0 copy-start.1
  80.2 23.2 %shard_map.83 = bf16[8,16,120,128]{3,2,1,0:T(8,128)(2,1)} custom-call(bf16[8,16,120,128]{3,2,1,0:T(8,128)(2,1)} %bitcast.20, bf16[3584,2048]{1,0:T(8,128)(2,1)} %bitcast.23, bf16[1024,3584]{1,0:T(8,128)(2,1)} %bitcast.24), custom_call_target="tpu_custom_call" | custom-call | flops 12683575296 | bytes 22020096 | tf_op jit(solution)/shard_map/pallas_call | solution.py:191
  103.4 13.3 %all-gather.3.cloned.1.call-done = bf16[3584,1024]{1,0:T(8,128)(2,1)} async-done(((bf16[224,1024]{1,0:T(8,128)(2,1)}), bf16[3584,1024]{1,0:T(8,128)(2,1)}) %all-gather.3.cloned.1.call-update) | async-done | bytes 7340048 | tf_op jit(solution)/shard_map/all_gather | solution.py:319
  116.7 0.0 copy-done.1
  116.7 5.2 %fusion = f32[256,1024]{1,0:T(8,128)S(1)} fusion(bf16[3584,1024]{1,0:T(8,128)(2,1)} %all-gather.3.cloned.1.call-done, bf16[448,8,2,128]{3,2,1,0:T(2,128)(2,1)S(1)} %bitcast.18), kind=kOutput, calls=%fused_computation | convolution fusion | flops 1879048192 | bytes 10223616 | tf_op jit(solution)/shard_map/dot_general | solution.py:27
  121.9 0.9 fusion.3
  122.8 0.0 all-gather.5.cloned.1.call-update
  122.8 8.3 %all-to-all-start.1 = ((bf16[128,120,128]{2,1,0:T(8,128)(2,1)}), bf16[128,120,128]{2,1,0:T(8,128)(2,1)}, u32[]{:S(2)}, u32[]{:S(2)}) async-start(bf16[128,120,128]{2,1,0:T(8,128)(2,1)} %bitcast.19), calls=%async_computation.1 | async-start | bytes 7864320 | tf_op jit(solution)/shard_map/all_to_all | solution.py:325
  131.1 10.5 %shard_map.84 = (bf16[1024,8192]{1,0:T(8,128)(2,1)}, bf16[1024,1024]{1,0:T(8,128)(2,1)}) custom-call(f32[128,1024]{1,0:T(8,128)} %get-tuple-element.12.rank_ref, f32[128,1024]{1,0:T(8,128)} %get-tuple-element.13.weight_ref), custom_call_target="tpu_custom_call" | custom-call | flops 16777216 | bytes 20000000 | tf_op jit(solution)/shard_map/pallas_call | solution.py:233
  141.7 63.2 %all-gather.5.cloned.1.call-done = bf16[2048,1024]{1,0:T(8,128)(2,1)} async-done(((bf16[128,1024]{1,0:T(8,128)(2,1)}), bf16[2048,1024]{1,0:T(8,128)(2,1)}) %all-gather.5.cloned.1.call-update) | async-done | bytes 4194320 | tf_op jit(solution)/shard_map/all_gather | solution.py:335
  204.8 0.0 copy-done
  204.8 4.2 %convolution_bitcast_fusion.shared_ref = f32[224,1024]{1,0:T(8,128)} fusion(bf16[2048,224]{0,1:T(8,128)(2,1)S(1)} %copy-done, bf16[2048,1024]{1,0:T(8,128)(2,1)} %all-gather.5.cloned.1.call-done), kind=kOutput, calls=%fused_computation.3 | convolution fusion | flops 939524096 | bytes 6029312 | tf_op jit(solution)/shard_map/dot_general | solution.py:27
  209.0 0.0 all-to-all-done.1.back_ref
  209.1 12.6 %shard_map.85 = bf16[224,1024]{1,0:T(8,128)(2,1)} custom-call(bf16[128,120,128]{2,1,0:T(8,128)(2,1)} %all-to-all-done.1.back_ref, bf16[1024,8192]{1,0:T(8,128)(2,1)} %get-tuple-element.14.main_ref, bf16[1024,1024]{1,0:T(8,128)(2,1)} %get-tuple-element.15.late_ref, f32[224,1024]{1,0:T(8,128)} %convolution_bitcast_fusion.shared_ref), custom_call_target="tpu_custom_call" | custom-call | flops 4831838208 | bytes 24000000 | tf_op jit(solution)/shard_map/pallas_call | solution.py:286
Async XLA Ops:
  6.5 198.3 %copy-start = (bf16[2048,224]{0,1:T(8,128)(2,1)S(1)}, bf16[2048,224]{0,1:T(8,128)(2,1)}, u32[]{:S(2)}) copy-start(bf16[2048,224]{0,1:T(8,128)(2,1)} %param.15) | copy-start | bytes 2752516
  6.5 110.2 %all-gather.3.cloned.1.call-start = ((), (), s32[]{:S(2)}) async-start(), calls=%async_computation.2 | async-start | bytes 7798784 | tf_op jit(solution)/shard_map/all_gather | solution.py:319
  7.3 197.5 %all-gather.5.cloned.1.call-start = ((), (), s32[]{:S(2)}) async-start(), calls=%async_computation.3 | async-start | bytes 4456448 | tf_op jit(solution)/shard_map/all_gather | solution.py:335
  80.2 36.6 %copy-start.1 = (bf16[3584,2,128]{2,1,0:T(2,128)(2,1)S(1)}, bf16[3584,2,128]{2,1,0:T(2,128)(2,1)}, u32[]{:S(2)}) copy-start(bf16[3584,2,128]{2,1,0:T(2,128)(2,1)} %param.14) | copy-start | bytes 5505028
  122.8 86.3 %all-to-all-start.1 = ((bf16[128,120,128]{2,1,0:T(8,128)(2,1)}), bf16[128,120,128]{2,1,0:T(8,128)(2,1)}, u32[]{:S(2)}, u32[]{:S(2)}) async-start(bf16[128,120,128]{2,1,0:T(8,128)(2,1)} %bitcast.19), calls=%async_computation.1 | async-start | bytes 7864320 | tf_op jit(solution)/shard_map/all_to_all | solution.py:325
Sparse Core Ops, SparseCore 0:
  9.5 107.1 all-gather.2
  122.9 81.8 all-gather.4
where the time goes:
time: 230 us; the launch traced here: 229 us
  waiting for transfers between devices  77.2 us (34%)
  blocking collectives  63.1 us (27%)
  Pallas kernels  56.2 us (24%)
  between operations  13.4 us (6%)
  matrix products  9.41 us (4%)
  starting transfers between devices  8.38 us (4%)
    all_gather x1, waiting for transfers between devices, on_device(): shared_all = lax.all_gather(shared_act, 'tp', axis=0, tiled=True)  63.2 us
    all_to_all x1, blocking collectives, exchange(): lax.all_to_all(blocks, ('dp', 'tp'), split_axis=0, concat_axis=0, tiled=T...  63.1 us
    pallas_call x1, Pallas kernels, expert(): pl.pallas_call(functools.partial(expert_kernel, tile), out_shape=jax.Shap...  23.2 us
    all_gather x1, waiting for transfers between devices, on_device(): features_all = lax.all_gather(features, 'tp', axis=0, tiled=True)  13.3 us
    pallas_call x1, Pallas kernels, combine(): pl.pallas_call(functools.partial(combine_kernel, steps), out_shape=jax.Sh...  12.6 us
    pallas_call x1, Pallas kernels, spread(): pl.pallas_call(spread_kernel, out_shape=(jax.ShapeDtypeStruct((tokens, ex...  10.5 us
    pallas_call x1, Pallas kernels, dispatch(): pl.pallas_call(functools.partial(dispatch_kernel, per_step), out_shape=(t...  9.81 us
    dot_general x2, matrix products, dot(): return lax.dot_general(a, b, (dims, ((), ())), preferred_element_type=F32)  9.41 us
  transfers between devices with their start and end apart: 3, of which 2 were waited for; matrix products, arithmetic and copies ran while one was open for 2% of the time, Pallas kernels for 19%

commit v1 on v0

--- a/solution.py
+++ b/solution.py
@@ -246,8 +246,9 @@
     )(rank, weight)
 
 
-def combine_kernel(steps, back_ref, main_ref, late_ref, shared_ref, out_ref, total):
+def combine_kernel(last, back_ref, main_ref, late_ref, *refs):
     step = pl.program_id(0)
+    total = refs[-1]
     line = lax.broadcasted_iota(jnp.int32, (8, 128), 0)
     left, right, extra_l, extra_r = [], [], [], []
     for e in range(back_ref.shape[0]):
@@ -266,40 +267,100 @@
 
     @pl.when(step == 0)
     def _():
-        total[...] = part
-
-    @pl.when((step > 0) & (step < steps - 1))
+        total[...] = part + refs[0][...] if last else part
+
+    @pl.when(step > 0)
     def _():
         total[...] += part
 
-    @pl.when(step == steps - 1)
-    def _():
-        feats = out_ref.shape[0]
-        out_ref[...] = ((total[...] + part).T[:feats] + shared_ref[...]).astype(BF16)
-
-
-def combine(back, main, late, shared, per_step=32):
+    if last:
+
+        @pl.when(step == pl.num_programs(0) - 1)
+        def _():
+            out_ref = refs[1]
+            out_ref[...] = total[...].T[: out_ref.shape[0]]
+
+
+def combine(back, main, late, feats, earlier=None, per_step=32):
     experts = back.shape[0]
     tokens = main.shape[0]
-    feats = shared.shape[0]
-    steps = experts // per_step
+    last = earlier is not None
+    steps = experts // per_step // 2
+    base = steps if last else 0
+    sums = pl.BlockSpec((tokens, 256), lambda i: (0, 0))
+    out = pl.BlockSpec((feats, tokens), lambda i: (0, 0)) if last else sums
     return pl.pallas_call(
-        functools.partial(combine_kernel, steps),
-        out_shape=jax.ShapeDtypeStruct((feats, tokens), BF16),
+        functools.partial(combine_kernel, last),
+        out_shape=jax.ShapeDtypeStruct((feats, tokens) if last else (tokens, 256), F32),
         grid=(steps,),
         in_specs=[
-            pl.BlockSpec((per_step, PACK, 128), lambda i: (i, 0, 0)),
-            pl.BlockSpec((tokens, per_step * 64), lambda i: (0, i)),
-            pl.BlockSpec((tokens, per_step * 8), lambda i: (0, i)),
-            pl.BlockSpec((feats, tokens), lambda i: (0, 0)),
-        ],
-        out_specs=pl.BlockSpec((feats, tokens), lambda i: (0, 0)),
-        scratch_shapes=[pltpu.VMEM((tokens, 256), F32)],
+            pl.BlockSpec((per_step, PACK, 128), lambda i: (i + base, 0, 0)),
+            pl.BlockSpec((tokens, per_step * 64), lambda i: (0, i + base)),
+            pl.BlockSpec((tokens, per_step * 8), lambda i: (0, i + base)),
+        ]
+        + [sums] * last,
+        out_specs=out,
+        scratch_shapes=[pltpu.VMEM((tokens, 256), F32)] * last,
         compiler_params=params(("arbitrary",), 56 * 1024 * 1024),
         cost_estimate=pl.CostEstimate(
-            flops=2 * experts * 72 * 256 * tokens, bytes_accessed=24 * 10**6, transcendentals=0
-        ),
-    )(back, main, late, shared)
+            flops=experts * 72 * 256 * tokens, bytes_accessed=12 * 10**6, transcendentals=0
+        ),
+    )(back, main, late, *([earlier] if last else []))
+
+
+def finish_kernel(count, weights_a_ref, weights_b_ref, routed_ref, *refs):
+    out_ref = refs[-1]
+    half = out_ref.shape[1] // 2
+    for i, weights_ref in enumerate((weights_a_ref, weights_b_ref)):
+        units = jnp.concatenate([r[...] for r in refs[i * count : (i + 1) * count]], axis=0)
+        cols = slice(i * half, (i + 1) * half)
+        out = dot(weights_ref[...], units, ((1,), (0,)))
+        out_ref[:, cols] = (out + routed_ref[:, cols]).astype(BF16)
+
+
+def finish(weights_a, weights_b, routed, parts_a, parts_b):
+    return pl.pallas_call(
+        functools.partial(finish_kernel, len(parts_a)),
+        out_shape=jax.ShapeDtypeStruct(routed.shape, BF16),
+        in_specs=[whole()] * (3 + len(parts_a) + len(parts_b)),
+        out_specs=whole(),
+        compiler_params=params(vmem=20 * 1024 * 1024),
+        cost_estimate=pl.CostEstimate(flops=10**9, bytes_accessed=7 * 10**6, transcendentals=0),
+    )(weights_a, weights_b, routed, *parts_a, *parts_b)
+
+
+def from_x(value, offset):
+    pairs = [
+        (y * SIDE + (x + offset) % SIDE, y * SIDE + x) for y in range(SIDE) for x in range(SIDE)
+    ]
+    return lax.ppermute(value, "tp", pairs)
+
+
+def from_y(value, offset):
+    pairs = [
+        ((y + offset) % SIDE * SIDE + x, y * SIDE + x) for y in range(SIDE) for x in range(SIDE)
+    ]
+    return lax.ppermute(value, "tp", pairs)
+
+
+OFFSETS = (0, 1, -1, 2)
+
+
+def gather_halves(value, first, beside):
+    half = value.shape[1] // 2
+    a, b = value[:, :half], value[:, half:]
+    line = [from_x(a, o) for o in OFFSETS[1:]] + [from_y(b, o) for o in OFFSETS[1:]]
+    line, first = lax.optimization_barrier((line, first))
+    a = jnp.concatenate([a] + line[:3], axis=0)
+    b = jnp.concatenate([b] + line[3:], axis=0)
+    near = (from_y(a, 1), from_y(a, -1), from_x(b, 1), from_x(b, -1))
+    extra = beside(first)
+    near, extra = lax.optimization_barrier((near, extra))
+    a_next, a_prev, b_next, b_prev = near
+    mid = a.shape[0] // 2
+    far_a = [from_y(a_prev[:mid], -1), from_y(a_next[mid:], 1)]
+    far_b = [from_x(b_prev[:mid], -1), from_x(b_next[mid:], 1)]
+    return [a, a_next, a_prev] + far_a, [b, b_next, b_prev] + far_b, extra
 
 
 def on_device(
@@ -327,17 +388,34 @@
     got = exchange(blocks).reshape(groups, n_tensor, PACK, 128)
     packed = expert(got, expert_gate_up[0], expert_down[0])
 
-    shared_gate_up, _ = lax.optimization_barrier((shared_gate_up, packed))
+    rank, shared_down, _ = lax.optimization_barrier((rank, shared_down, packed))
+    mine = lax.axis_index("tp")
+    my_y, my_x = mine // SIDE, mine % SIDE
+    ys = [(my_y + o) % SIDE * SIDE for o in OFFSETS]
+    xs = [(my_x + o) % SIDE for o in OFFSETS]
+    weights = shared_down.T.reshape(-1, n_tensor, shared_down.shape[0] // n_tensor)
+    order_a = jnp.stack([y + x for y in ys for x in xs])
+    order_b = jnp.stack([y + x for x in xs for y in ys])
+    weights_a = jnp.take(weights, order_a, axis=1, mode="clip").reshape(weights.shape[0], -1)
+    weights_b = jnp.take(weights, order_b, axis=1, mode="clip").reshape(weights.shape[0], -1)
+    main, late = spread(rank, weight)
+    back = exchange(packed.reshape(experts, PACK, 128))
+
+    shared_gate_up, weights_a, weights_b, _ = lax.optimization_barrier(
+        (shared_gate_up, weights_a, weights_b, late)
+    )
     shared_w = shared_gate_up.reshape(features_all.shape[0], -1)
     proj = dot(shared_w, features_all, ((0,), (0,)))
     units = proj.shape[0] // 2
     shared_act = (jax.nn.silu(proj[:units]) * proj[units:]).astype(BF16)
-    shared_all = lax.all_gather(shared_act, "tp", axis=0, tiled=True)
-
-    main, late = spread(rank, weight)
-    back = exchange(packed.reshape(experts, PACK, 128))
-    shared_out = dot(shared_down.T, shared_all, ((1,), (0,)))
-    return combine(back, main, late, shared_out).T
+
+    feats = features.shape[0]
+    parts_a, parts_b, routed = gather_halves(
+        shared_act,
+        combine(back, main, late, feats),
+        lambda earlier: combine(back, main, late, feats, earlier),
+    )
+    return finish(weights_a, weights_b, routed, parts_a, parts_b).T
 
 
 def solution(mesh):

time: 230 us -> 210 us (0.913)
  waiting for transfers between devices: 77.2 us -> 22.2 us
  starting transfers between devices: 8.38 us -> 38.7 us
  local copies, waits for them, and re-layouts: 0.01 us -> 5.37 us
  Pallas kernels: 56.2 us -> 60.7 us
  matrix products: 9.41 us -> 5.73 us
    all_gather x1 -> x0, waiting for transfers between devices: 63.2 us -> none  [on_device(): shared_all = lax.all_gather(shared_act, 'tp', axis=0, tiled=True)]
    ppermute x0 -> x14, starting transfers between devices: none -> 32 us  [the longest x7 16.6 us: from_x(): return lax.ppermute(value, 'tp', pairs)]
    ppermute x0 -> x14, waiting for transfers between devices: none -> 11 us  [the longest x7 8.33 us: from_y(): return lax.ppermute(value, 'tp', pairs)]
    pallas_call x1 -> x3, Pallas kernels: 12.6 us -> 17.3 us  [the longest x2 15.4 us: combine(): pl.pallas_call(functools.partial(combine_kernel, last), out_shape=jax.Sha...]
    dot_general x2 -> x1, matrix products: 9.41 us -> 5.73 us  [dot(): return lax.dot_general(a, b, (dims, ((), ())), preferred_element_type=F32)]
    all_gather x1, waiting for transfers between devices: 13.3 us -> 10.4 us  [on_device(): features_all = lax.all_gather(features, 'tp', axis=0, tiled=True)]
    gather x0 -> x2, local copies, waits for them, and re-layouts: none -> 2.33 us  [the longest x1 1.61 us: on_device(): jnp.take(weights, order_a, axis=1, mode='clip')]
  transfers between devices with their start and end apart: 3 -> 16, of which waited for: 2 -> 8; matrix products, arithmetic and copies ran while one was open for 2% -> 5% of each run, Pallas kernels for 19% -> 28%
where the time goes in v1:
time: 210 us
  blocking collectives  63 us (30%)
  Pallas kernels  60.7 us (29%)
  starting transfers between devices  38.7 us (18%)
  waiting for transfers between devices  22.2 us (11%)
  between operations  13.7 us (7%)
  matrix products  5.73 us (3%)
  local copies, waits for them, and re-layouts  5.37 us (3%)
    all_to_all x1, blocking collectives, exchange(): lax.all_to_all(blocks, ('dp', 'tp'), split_axis=0, concat_axis=0, tiled=T...  63 us
    pallas_call x1, Pallas kernels, expert(): pl.pallas_call(functools.partial(expert_kernel, tile), out_shape=jax.Shap...  23.1 us
    ppermute x7, starting transfers between devices, from_x(): return lax.ppermute(value, 'tp', pairs)  16.6 us
    ppermute x7, starting transfers between devices, from_y(): return lax.ppermute(value, 'tp', pairs)  15.4 us
    pallas_call x2, Pallas kernels, combine(): pl.pallas_call(functools.partial(combine_kernel, last), out_shape=jax.Sha...  15.4 us
    pallas_call x1, Pallas kernels, spread(): pl.pallas_call(spread_kernel, out_shape=(jax.ShapeDtypeStruct((tokens, ex...  10.6 us
    all_gather x1, waiting for transfers between devices, on_device(): features_all = lax.all_gather(features, 'tp', axis=0, tiled=True)  10.4 us
    pallas_call x1, Pallas kernels, dispatch(): pl.pallas_call(functools.partial(dispatch_kernel, per_step), out_shape=(t...  9.8 us
  transfers between devices with their start and end apart: 16, of which 8 were waited for; matrix products, arithmetic and copies ran while one was open for 5% of the time, Pallas kernels for 28%

profile of v1, /device:TPU:24, one launch (start us, length us, event | category | flops | bytes accessed | tf_op | source)
XLA Modules:
  0.0 209.6 jit_solution(9426295579638100291)
XLA Ops:
  6.5 0.7 all-gather.2.cloned.1.call-update
  7.3 9.8 %shard_map.82 = (f32[128,1024]{1,0:T(8,128)}, f32[128,1024]{1,0:T(8,128)}, bf16[128,120,128]{2,1,0:T(8,128)(2,1)}) custom-call(s32[8,1024]{1,0:T(8,128)} %bitcast.55, f32[8,1024]{1,0:T(8,128)} %bitcast.56, s32[1,128]{1,0:T(1,128)} %bitcast.57, bf16[224,1024]{1,0:T(8,128)(2,1)} %bitcast.52), custom_call_target="tpu_custom_call" | custom-call | flops 4831838208 | bytes 6000000 | tf_op jit(solution)/shard_map/pallas_call | solution.py:96
  17.1 63.0 %all_to_all.10 = bf16[128,120,128]{2,1,0:T(8,128)(2,1)} all-to-all(bf16[128,120,128]{2,1,0:T(8,128)(2,1)} %get-tuple-element.28), channel_id=1, replica_groups=mesh['dp'=8,'tp'=16] {'dp','tp'}, dimensions={0} | all-to-all | bytes 7864320 | tf_op jit(solution)/shard_map/all_to_all | solution.py:386
  80.0 23.1 %shard_map.83 = bf16[8,16,120,128]{3,2,1,0:T(8,128)(2,1)} custom-call(bf16[8,16,120,128]{3,2,1,0:T(8,128)(2,1)} %bitcast.50, bf16[3584,2048]{1,0:T(8,128)(2,1)} %bitcast.53, bf16[1024,3584]{1,0:T(8,128)(2,1)} %bitcast.54), custom_call_target="tpu_custom_call" | custom-call | flops 12683575296 | bytes 22020096 | tf_op jit(solution)/shard_map/pallas_call | solution.py:191
  103.1 6.6 %all-to-all-start.1 = ((bf16[128,120,128]{2,1,0:T(8,128)(2,1)}), bf16[128,120,128]{2,1,0:T(8,128)(2,1)}, u32[]{:S(2)}, u32[]{:S(2)}) async-start(bf16[128,120,128]{2,1,0:T(8,128)(2,1)} %bitcast.49), calls=%async_computation.1 | async-start | bytes 7864320 | tf_op jit(solution)/shard_map/all_to_all | solution.py:386
  110.3 0.7 gather_fusion.1
  111.0 1.6 gather_fusion
  112.6 10.6 %shard_map.84 = (bf16[1024,8192]{1,0:T(8,128)(2,1)}, bf16[1024,1024]{1,0:T(8,128)(2,1)}) custom-call(f32[128,1024]{1,0:T(8,128)} %get-tuple-element.30.rank_ref, f32[128,1024]{1,0:T(8,128)} %get-tuple-element.31.weight_ref), custom_call_target="tpu_custom_call" | custom-call | flops 16777216 | bytes 20000000 | tf_op jit(solution)/shard_map/pallas_call | solution.py:233
  123.2 1.4 copy_bitcast_fusion
  124.6 10.4 %all-gather.2.cloned.1.call-done = bf16[3584,1024]{1,0:T(8,128)(2,1)} async-done(((bf16[224,1024]{1,0:T(8,128)(2,1)}), bf16[3584,1024]{1,0:T(8,128)(2,1)}) %all-gather.2.cloned.1.call-update) | async-done | bytes 7340048 | tf_op jit(solution)/shard_map/all_gather | solution.py:380
  135.1 5.7 %fusion = f32[256,1024]{1,0:T(8,128)S(1)} fusion(bf16[3584,1024]{1,0:T(8,128)(2,1)} %all-gather.2.cloned.1.call-done, bf16[448,8,2,128]{3,2,1,0:T(2,128)(2,1)} %bitcast.48), kind=kOutput, calls=%fused_computation.2 | convolution fusion | flops 1879048192 | bytes 10223616 | tf_op jit(solution)/shard_map/dot_general | solution.py:27
  141.0 8.9 %collective-permute-start.5 = (bf16[128,512]{1,0:T(8,128)(2,1)S(1)}, bf16[128,512]{1,0:T(8,128)(2,1)S(1)}, u32[]{:S(2)}, u32[]{:S(2)}) collective-permute-start(bf16[128,512]{1,0:T(8,128)(2,1)S(1)} %get-tuple-element.49), channel_id=1, source_target_pairs={{8,0},{9,1},{10,2},{11,3},{12,4},{13,5},{14,6},{15,7},{0,8},{1,9},... | collective-permute-start | bytes 393224 | tf_op jit(solution)/shard_map/ppermute | solution.py:343
  149.9 0.2 collective-permute-start.4
  150.1 1.9 collective-permute-start.3
  151.9 7.2 %collective-permute-start.2 = (bf16[128,512]{1,0:T(8,128)(2,1)S(1)}, bf16[128,512]{1,0:T(8,128)(2,1)S(1)}, u32[]{:S(2)}, u32[]{:S(2)}) collective-permute-start(bf16[128,512]{1,0:T(8,128)(2,1)S(1)} %get-tuple-element.50), channel_id=1, source_target_pairs={{2,0},{3,1},{0,2},{1,3},{6,4},{7,5},{4,6},{5,7},{10,8},{11,9},{8,1... | collective-permute-start | bytes 393224 | tf_op jit(solution)/shard_map/ppermute | solution.py:336
  159.1 0.9 collective-permute-done.5
  160.0 2.8 %collective-permute-start = (bf16[128,512]{1,0:T(8,128)(2,1)S(1)}, bf16[128,512]{1,0:T(8,128)(2,1)S(1)}, u32[]{:S(2)}, u32[]{:S(2)}) collective-permute-start(bf16[128,512]{1,0:T(8,128)(2,1)S(1)} %get-tuple-element.50), channel_id=1, source_target_pairs={{1,0},{2,1},{3,2},{0,3},{5,4},{6,5},{7,6},{4,7},{9,8},{10,9},{11,1... | collective-permute-start | bytes 393224 | tf_op jit(solution)/shard_map/ppermute | solution.py:336
  162.9 6.8 %shard_map.85.refs_0_ = f32[1024,256]{1,0:T(8,128)} custom-call(bf16[128,120,128]{2,1,0:T(8,128)(2,1)} %all-to-all-done.1.back_ref, bf16[1024,8192]{1,0:T(8,128)(2,1)} %get-tuple-element.36.main_ref, bf16[1024,1024]{1,0:T(8,128)(2,1)} %get-tuple-element.32.late_ref), custom_call_target="tpu_custom_call" | custom-call | flops 2415919104 | bytes 12000000 | tf_op jit(solution)/shard_map/pallas_call | solution.py:292
  169.8 3.2 %collective-permute-start.8 = (bf16[512,512]{1,0:T(8,128)(2,1)S(1)}, bf16[512,512]{1,0:T(8,128)(2,1)S(1)}, u32[]{:S(2)}, u32[]{:S(2)}) collective-permute-start(bf16[512,512]{1,0:T(8,128)(2,1)S(1)} %pad_maximum_fusion.1.refs_5_), channel_id=1, source_target_pairs={{1,0},{2,1},{3,2},{0,3},{5,4},{6,5},{7,6},{4,7},{9,8},{10,9},{11,1... | collective-permute-start | bytes 1572872 | tf_op jit(solution)/shard_map/ppermute | solution.py:336
  173.1 2.4 %collective-permute-start.7 = (bf16[512,512]{1,0:T(8,128)(2,1)S(1)}, bf16[512,512]{1,0:T(8,128)(2,1)S(1)}, u32[]{:S(2)}, u32[]{:S(2)}) collective-permute-start(bf16[512,512]{1,0:T(8,128)(2,1)S(1)} %pad_maximum_fusion.refs_0_), channel_id=1, source_target_pairs={{12,0},{13,1},{14,2},{15,3},{0,4},{1,5},{2,6},{3,7},{4,8},{5,9},{6... | collective-permute-start | bytes 1572872 | tf_op jit(solution)/shard_map/ppermute | solution.py:343
  175.6 8.6 %shard_map.86.routed_ref = f32[224,1024]{1,0:T(8,128)} custom-call(bf16[128,120,128]{2,1,0:T(8,128)(2,1)} %all-to-all-done.1.back_ref, bf16[1024,8192]{1,0:T(8,128)(2,1)} %get-tuple-element.36.main_ref, bf16[1024,1024]{1,0:T(8,128)(2,1)} %get-tuple-element.32.late_ref, f32[1024,256]{1,0:T(8,128)} %shard_map.85.refs_0_), custom_call_target="tpu_custom_call" | custom-call | flops 2415919104 | bytes 12000000 | tf_op jit(solution)/shard_map/pallas_call | solution.py:292
  184.1 0.4 collective-permute-done.9.refs_7_
  184.5 1.6 collective-permute-done.7.refs_2_
  186.1 2.3 %collective-permute-done.6.refs_1_ = bf16[512,512]{1,0:T(8,128)(2,1)S(1)} collective-permute-done((bf16[512,512]{1,0:T(8,128)(2,1)S(1)}, bf16[512,512]{1,0:T(8,128)(2,1)S(1)}, u32[]{:S(2)}, u32[]{:S(2)}) %collective-permute-start.6) | collective-permute-done | bytes 524320 | tf_op jit(solution)/shard_map/ppermute | solution.py:343
  188.6 3.2 %collective-permute-start.13 = (bf16[256,512]{1,0:T(8,128)(2,1)S(1)}, bf16[256,512]{1,0:T(8,128)(2,1)S(1)}, u32[]{:S(2)}, u32[]{:S(2)}) collective-permute-start(bf16[256,512]{1,0:T(8,128)(2,1)S(1)} %slice.31), channel_id=1, source_target_pairs={{1,0},{2,1},{3,2},{0,3},{5,4},{6,5},{7,6},{4,7},{9,8},{10,9},{11,1... | collective-permute-start | bytes 786440 | tf_op jit(solution)/shard_map/ppermute | solution.py:336
  191.8 0.3 collective-permute-start.10
  192.1 1.7 collective-permute-start.11
  193.9 2.3 %collective-permute-done.12.refs_8_ = bf16[256,512]{1,0:T(8,128)(2,1)S(1)} collective-permute-done((bf16[256,512]{1,0:T(8,128)(2,1)S(1)}, bf16[256,512]{1,0:T(8,128)(2,1)S(1)}, u32[]{:S(2)}, u32[]{:S(2)}) %collective-permute-start.12) | collective-permute-done | bytes 262176 | tf_op jit(solution)/shard_map/ppermute | solution.py:336
  196.2 2.0 collective-permute-done.10.refs_3_
  198.2 1.5 collective-permute-done.11.refs_4_
  199.7 1.2 copy-done.2
  200.9 1.9 shard_map.87
  (31 shorter events, 0.9 us)
Async XLA Ops:
  6.5 103.6 %copy-start = (bf16[2048,224]{0,1:T(8,128)(2,1)S(1)}, bf16[2048,224]{0,1:T(8,128)(2,1)}, u32[]{:S(2)}) copy-start(bf16[2048,224]{0,1:T(8,128)(2,1)} %param.15) | copy-start | bytes 2752516
  6.5 128.5 %all-gather.2.cloned.1.call-start = ((), (), s32[]{:S(2)}) async-start(), calls=%async_computation.2 | async-start | bytes 7798784 | tf_op jit(solution)/shard_map/all_gather | solution.py:380
  103.1 59.8 %all-to-all-start.1 = ((bf16[128,120,128]{2,1,0:T(8,128)(2,1)}), bf16[128,120,128]{2,1,0:T(8,128)(2,1)}, u32[]{:S(2)}, u32[]{:S(2)}) async-start(bf16[128,120,128]{2,1,0:T(8,128)(2,1)} %bitcast.49), calls=%async_computation.1 | async-start | bytes 7864320 | tf_op jit(solution)/shard_map/all_to_all | solution.py:386
  141.0 19.1 %collective-permute-start.5 = (bf16[128,512]{1,0:T(8,128)(2,1)S(1)}, bf16[128,512]{1,0:T(8,128)(2,1)S(1)}, u32[]{:S(2)}, u32[]{:S(2)}) collective-permute-start(bf16[128,512]{1,0:T(8,128)(2,1)S(1)} %get-tuple-element.49), channel_id=1, source_target_pairs={{8,0},{9,1},{10,2},{11,3},{12,4},{13,5},{14,6},{15,7},{0,8},{1,9},... | collective-permute-start | bytes 393224 | tf_op jit(solution)/shard_map/ppermute | solution.py:343
  149.9 19.8 %collective-permute-start.4 = (bf16[128,512]{1,0:T(8,128)(2,1)S(1)}, bf16[128,512]{1,0:T(8,128)(2,1)S(1)}, u32[]{:S(2)}, u32[]{:S(2)}) collective-permute-start(bf16[128,512]{1,0:T(8,128)(2,1)S(1)} %get-tuple-element.49), channel_id=1, source_target_pairs={{12,0},{13,1},{14,2},{15,3},{0,4},{1,5},{2,6},{3,7},{4,8},{5,9},{6... | collective-permute-start | bytes 393224 | tf_op jit(solution)/shard_map/ppermute | solution.py:343
  150.1 19.6 %collective-permute-start.3 = (bf16[128,512]{1,0:T(8,128)(2,1)S(1)}, bf16[128,512]{1,0:T(8,128)(2,1)S(1)}, u32[]{:S(2)}, u32[]{:S(2)}) collective-permute-start(bf16[128,512]{1,0:T(8,128)(2,1)S(1)} %get-tuple-element.49), channel_id=1, source_target_pairs={{4,0},{5,1},{6,2},{7,3},{8,4},{9,5},{10,6},{11,7},{12,8},{13,9},{1... | collective-permute-start | bytes 393224 | tf_op jit(solution)/shard_map/ppermute | solution.py:343
  151.9 17.8 %collective-permute-start.2 = (bf16[128,512]{1,0:T(8,128)(2,1)S(1)}, bf16[128,512]{1,0:T(8,128)(2,1)S(1)}, u32[]{:S(2)}, u32[]{:S(2)}) collective-permute-start(bf16[128,512]{1,0:T(8,128)(2,1)S(1)} %get-tuple-element.50), channel_id=1, source_target_pairs={{2,0},{3,1},{0,2},{1,3},{6,4},{7,5},{4,6},{5,7},{10,8},{11,9},{8,1... | collective-permute-start | bytes 393224 | tf_op jit(solution)/shard_map/ppermute | solution.py:336
  159.1 10.6 %collective-permute-start.1 = (bf16[128,512]{1,0:T(8,128)(2,1)S(1)}, bf16[128,512]{1,0:T(8,128)(2,1)S(1)}, u32[]{:S(2)}, u32[]{:S(2)}) collective-permute-start(bf16[128,512]{1,0:T(8,128)(2,1)S(1)} %get-tuple-element.50), channel_id=1, source_target_pairs={{3,0},{0,1},{1,2},{2,3},{7,4},{4,5},{5,6},{6,7},{11,8},{8,9},{9,10... | collective-permute-start | bytes 393224 | tf_op jit(solution)/shard_map/ppermute | solution.py:336
  160.0 9.7 %collective-permute-start = (bf16[128,512]{1,0:T(8,128)(2,1)S(1)}, bf16[128,512]{1,0:T(8,128)(2,1)S(1)}, u32[]{:S(2)}, u32[]{:S(2)}) collective-permute-start(bf16[128,512]{1,0:T(8,128)(2,1)S(1)} %get-tuple-element.50), channel_id=1, source_target_pairs={{1,0},{2,1},{3,2},{0,3},{5,4},{6,5},{7,6},{4,7},{9,8},{10,9},{11,1... | collective-permute-start | bytes 393224 | tf_op jit(solution)/shard_map/ppermute | solution.py:336
  169.8 14.8 %collective-permute-start.9 = (bf16[512,512]{1,0:T(8,128)(2,1)S(1)}, bf16[512,512]{1,0:T(8,128)(2,1)S(1)}, u32[]{:S(2)}, u32[]{:S(2)}) collective-permute-start(bf16[512,512]{1,0:T(8,128)(2,1)S(1)} %pad_maximum_fusion.1.refs_5_), channel_id=1, source_target_pairs={{3,0},{0,1},{1,2},{2,3},{7,4},{4,5},{5,6},{6,7},{11,8},{8,9},{9,10... | collective-permute-start | bytes 1572872 | tf_op jit(solution)/shard_map/ppermute | solution.py:336
  169.8 14.7 %collective-permute-start.8 = (bf16[512,512]{1,0:T(8,128)(2,1)S(1)}, bf16[512,512]{1,0:T(8,128)(2,1)S(1)}, u32[]{:S(2)}, u32[]{:S(2)}) collective-permute-start(bf16[512,512]{1,0:T(8,128)(2,1)S(1)} %pad_maximum_fusion.1.refs_5_), channel_id=1, source_target_pairs={{1,0},{2,1},{3,2},{0,3},{5,4},{6,5},{7,6},{4,7},{9,8},{10,9},{11,1... | collective-permute-start | bytes 1572872 | tf_op jit(solution)/shard_map/ppermute | solution.py:336
  173.1 13.0 %collective-permute-start.7 = (bf16[512,512]{1,0:T(8,128)(2,1)S(1)}, bf16[512,512]{1,0:T(8,128)(2,1)S(1)}, u32[]{:S(2)}, u32[]{:S(2)}) collective-permute-start(bf16[512,512]{1,0:T(8,128)(2,1)S(1)} %pad_maximum_fusion.refs_0_), channel_id=1, source_target_pairs={{12,0},{13,1},{14,2},{15,3},{0,4},{1,5},{2,6},{3,7},{4,8},{5,9},{6... | collective-permute-start | bytes 1572872 | tf_op jit(solution)/shard_map/ppermute | solution.py:343
  175.5 12.9 %collective-permute-start.6 = (bf16[512,512]{1,0:T(8,128)(2,1)S(1)}, bf16[512,512]{1,0:T(8,128)(2,1)S(1)}, u32[]{:S(2)}, u32[]{:S(2)}) collective-permute-start(bf16[512,512]{1,0:T(8,128)(2,1)S(1)} %pad_maximum_fusion.refs_0_), channel_id=1, source_target_pairs={{4,0},{5,1},{6,2},{7,3},{8,4},{9,5},{10,6},{11,7},{12,8},{13,9},{1... | collective-permute-start | bytes 1572872 | tf_op jit(solution)/shard_map/ppermute | solution.py:343
  188.5 14.3 %copy-start.1 = (bf16[2048,224]{0,1:T(8,128)(2,1)S(1)}, bf16[2048,224]{0,1:T(8,128)(2,1)}, u32[]{:S(2)}) copy-start(bf16[2048,224]{0,1:T(8,128)(2,1)} %param.15) | copy-start | bytes 2752516
  188.5 7.7 %collective-permute-start.12 = (bf16[256,512]{1,0:T(8,128)(2,1)S(1)}, bf16[256,512]{1,0:T(8,128)(2,1)S(1)}, u32[]{:S(2)}, u32[]{:S(2)}) collective-permute-start(bf16[256,512]{1,0:T(8,128)(2,1)S(1)} %slice.30), channel_id=1, source_target_pairs={{3,0},{0,1},{1,2},{2,3},{7,4},{4,5},{5,6},{6,7},{11,8},{8,9},{9,10... | collective-permute-start | bytes 786440 | tf_op jit(solution)/shard_map/ppermute | solution.py:336
  188.6 7.6 %collective-permute-start.13 = (bf16[256,512]{1,0:T(8,128)(2,1)S(1)}, bf16[256,512]{1,0:T(8,128)(2,1)S(1)}, u32[]{:S(2)}, u32[]{:S(2)}) collective-permute-start(bf16[256,512]{1,0:T(8,128)(2,1)S(1)} %slice.31), channel_id=1, source_target_pairs={{1,0},{2,1},{3,2},{0,3},{5,4},{6,5},{7,6},{4,7},{9,8},{10,9},{11,1... | collective-permute-start | bytes 786440 | tf_op jit(solution)/shard_map/ppermute | solution.py:336
  191.8 6.4 %collective-permute-start.10 = (bf16[256,512]{1,0:T(8,128)(2,1)S(1)}, bf16[256,512]{1,0:T(8,128)(2,1)S(1)}, u32[]{:S(2)}, u32[]{:S(2)}) collective-permute-start(bf16[256,512]{1,0:T(8,128)(2,1)S(1)} %slice.28), channel_id=1, source_target_pairs={{12,0},{13,1},{14,2},{15,3},{0,4},{1,5},{2,6},{3,7},{4,8},{5,9},{6... | collective-permute-start | bytes 786440 | tf_op jit(solution)/shard_map/ppermute | solution.py:343
  192.1 7.6 %collective-permute-start.11 = (bf16[256,512]{1,0:T(8,128)(2,1)S(1)}, bf16[256,512]{1,0:T(8,128)(2,1)S(1)}, u32[]{:S(2)}, u32[]{:S(2)}) collective-permute-start(bf16[256,512]{1,0:T(8,128)(2,1)S(1)} %slice.29), channel_id=1, source_target_pairs={{4,0},{5,1},{6,2},{7,3},{8,4},{9,5},{10,6},{11,7},{12,8},{13,9},{1... | collective-permute-start | bytes 786440 | tf_op jit(solution)/shard_map/ppermute | solution.py:343
  199.7 1.2 copy-start.2
Sparse Core Ops, SparseCore 0:
  9.5 125.5 all-gather.1

commit v2 on v1

--- a/solution.py
+++ b/solution.py
@@ -246,9 +246,8 @@
     )(rank, weight)
 
 
-def combine_kernel(last, back_ref, main_ref, late_ref, *refs):
+def combine_kernel(steps, back_ref, main_ref, late_ref, out_ref, total):
     step = pl.program_id(0)
-    total = refs[-1]
     line = lax.broadcasted_iota(jnp.int32, (8, 128), 0)
     left, right, extra_l, extra_r = [], [], [], []
     for e in range(back_ref.shape[0]):
@@ -267,63 +266,61 @@
 
     @pl.when(step == 0)
     def _():
-        total[...] = part + refs[0][...] if last else part
-
-    @pl.when(step > 0)
+        total[...] = part
+
+    @pl.when((step > 0) & (step < steps - 1))
     def _():
         total[...] += part
 
-    if last:
-
-        @pl.when(step == pl.num_programs(0) - 1)
-        def _():
-            out_ref = refs[1]
-            out_ref[...] = total[...].T[: out_ref.shape[0]]
-
-
-def combine(back, main, late, feats, earlier=None, per_step=32):
+    @pl.when(step == steps - 1)
+    def _():
+        feats = out_ref.shape[0]
+        out_ref[...] = (total[...] + part).T[:feats]
+
+
+def combine(back, main, late, feats, per_step=32):
     experts = back.shape[0]
     tokens = main.shape[0]
-    last = earlier is not None
-    steps = experts // per_step // 2
-    base = steps if last else 0
-    sums = pl.BlockSpec((tokens, 256), lambda i: (0, 0))
-    out = pl.BlockSpec((feats, tokens), lambda i: (0, 0)) if last else sums
+    steps = experts // per_step
     return pl.pallas_call(
-        functools.partial(combine_kernel, last),
-        out_shape=jax.ShapeDtypeStruct((feats, tokens) if last else (tokens, 256), F32),
+        functools.partial(combine_kernel, steps),
+        out_shape=jax.ShapeDtypeStruct((feats, tokens), F32),
         grid=(steps,),
         in_specs=[
-            pl.BlockSpec((per_step, PACK, 128), lambda i: (i + base, 0, 0)),
-            pl.BlockSpec((tokens, per_step * 64), lambda i: (0, i + base)),
-            pl.BlockSpec((tokens, per_step * 8), lambda i: (0, i + base)),
-        ]
-        + [sums] * last,
-        out_specs=out,
-        scratch_shapes=[pltpu.VMEM((tokens, 256), F32)] * last,
+            pl.BlockSpec((per_step, PACK, 128), lambda i: (i, 0, 0)),
+            pl.BlockSpec((tokens, per_step * 64), lambda i: (0, i)),
+            pl.BlockSpec((tokens, per_step * 8), lambda i: (0, i)),
+        ],
+        out_specs=pl.BlockSpec((feats, tokens), lambda i: (0, 0)),
+        scratch_shapes=[pltpu.VMEM((tokens, 256), F32)],
         compiler_params=params(("arbitrary",), 56 * 1024 * 1024),
         cost_estimate=pl.CostEstimate(
-            flops=experts * 72 * 256 * tokens, bytes_accessed=12 * 10**6, transcendentals=0
-        ),
-    )(back, main, late, *([earlier] if last else []))
+            flops=2 * experts * 72 * 256 * tokens, bytes_accessed=24 * 10**6, transcendentals=0
+        ),
+    )(back, main, late)
 
 
 def finish_kernel(count, weights_a_ref, weights_b_ref, routed_ref, *refs):
-    out_ref = refs[-1]
+    out_ref, routed, sem = refs[-3:]
     half = out_ref.shape[1] // 2
+    copy = pltpu.make_async_copy(routed_ref, routed, sem)
+    copy.start()
     for i, weights_ref in enumerate((weights_a_ref, weights_b_ref)):
         units = jnp.concatenate([r[...] for r in refs[i * count : (i + 1) * count]], axis=0)
         cols = slice(i * half, (i + 1) * half)
         out = dot(weights_ref[...], units, ((1,), (0,)))
-        out_ref[:, cols] = (out + routed_ref[:, cols]).astype(BF16)
+        if i == 0:
+            copy.wait()
+        out_ref[:, cols] = (out + routed[:, cols]).astype(BF16)
 
 
 def finish(weights_a, weights_b, routed, parts_a, parts_b):
     return pl.pallas_call(
         functools.partial(finish_kernel, len(parts_a)),
         out_shape=jax.ShapeDtypeStruct(routed.shape, BF16),
-        in_specs=[whole()] * (3 + len(parts_a) + len(parts_b)),
+        in_specs=[whole(), whole(), whole(pl.ANY)] + [whole()] * (len(parts_a) + len(parts_b)),
         out_specs=whole(),
+        scratch_shapes=[pltpu.VMEM(routed.shape, F32), pltpu.SemaphoreType.DMA],
         compiler_params=params(vmem=20 * 1024 * 1024),
         cost_estimate=pl.CostEstimate(flops=10**9, bytes_accessed=7 * 10**6, transcendentals=0),
     )(weights_a, weights_b, routed, *parts_a, *parts_b)
@@ -346,16 +343,15 @@
 OFFSETS = (0, 1, -1, 2)
 
 
-def gather_halves(value, first, beside):
+def gather_halves(value, beside):
     half = value.shape[1] // 2
     a, b = value[:, :half], value[:, half:]
     line = [from_x(a, o) for o in OFFSETS[1:]] + [from_y(b, o) for o in OFFSETS[1:]]
-    line, first = lax.optimization_barrier((line, first))
+    line = lax.optimization_barrier(line)
     a = jnp.concatenate([a] + line[:3], axis=0)
     b = jnp.concatenate([b] + line[3:], axis=0)
     near = (from_y(a, 1), from_y(a, -1), from_x(b, 1), from_x(b, -1))
-    extra = beside(first)
-    near, extra = lax.optimization_barrier((near, extra))
+    near, extra = lax.optimization_barrier((near, beside(line[0])))
     a_next, a_prev, b_next, b_prev = near
     mid = a.shape[0] // 2
     far_a = [from_y(a_prev[:mid], -1), from_y(a_next[mid:], 1)]
@@ -409,12 +405,11 @@
     units = proj.shape[0] // 2
     shared_act = (jax.nn.silu(proj[:units]) * proj[units:]).astype(BF16)
 
-    feats = features.shape[0]
-    parts_a, parts_b, routed = gather_halves(
-        shared_act,
-        combine(back, main, late, feats),
-        lambda earlier: combine(back, main, late, feats, earlier),
-    )
+    def beside(arrived):
+        weights, _ = lax.optimization_barrier((late, arrived))
+        return combine(back, main, weights, features.shape[0])
+
+    parts_a, parts_b, routed = gather_halves(shared_act, beside)
     return finish(weights_a, weights_b, routed, parts_a, parts_b).T
 
 

time: 210 us -> 215 us (1.024)
  local copies, waits for them, and re-layouts: 5.37 us -> 10.3 us
    pallas_call x2 -> x1, Pallas kernels: 15.4 us -> 11.3 us  [combine(): pl.pallas_call(functools.partial(combine_kernel, steps), out_shape=jax.Sh...]
    ppermute x7, waiting for transfers between devices: 2.71 us -> 5.39 us  [from_x(): return lax.ppermute(value, 'tp', pairs)]
  transfers between devices with their start and end apart: 16 -> 16, of which waited for: 8 -> 8; matrix products, arithmetic and copies ran while one was open for 5% -> 6% of each run, Pallas kernels for 28% -> 26%
where the time goes in v2:
time: 215 us; the launch traced here: 214 us
  blocking collectives  63 us (29%)
  Pallas kernels  58.7 us (27%)
  starting transfers between devices  38.6 us (18%)
  waiting for transfers between devices  22.8 us (11%)
  between operations  13.7 us (6%)
  local copies, waits for them, and re-layouts  10.3 us (5%)
  matrix products  5.73 us (3%)
    all_to_all x1, blocking collectives, exchange(): lax.all_to_all(blocks, ('dp', 'tp'), split_axis=0, concat_axis=0, tiled=T...  63 us
    pallas_call x1, Pallas kernels, expert(): pl.pallas_call(functools.partial(expert_kernel, tile), out_shape=jax.Shap...  23.1 us
    ppermute x7, starting transfers between devices, from_x(): return lax.ppermute(value, 'tp', pairs)  17 us
    ppermute x7, starting transfers between devices, from_y(): return lax.ppermute(value, 'tp', pairs)  15 us
    pallas_call x1, Pallas kernels, combine(): pl.pallas_call(functools.partial(combine_kernel, steps), out_shape=jax.Sh...  11.3 us
    pallas_call x1, Pallas kernels, spread(): pl.pallas_call(spread_kernel, out_shape=(jax.ShapeDtypeStruct((tokens, ex...  10.6 us
    pallas_call x1, Pallas kernels, dispatch(): pl.pallas_call(functools.partial(dispatch_kernel, per_step), out_shape=(t...  9.81 us
    all_gather x1, waiting for transfers between devices, on_device(): features_all = lax.all_gather(features, 'tp', axis=0, tiled=True)  9.37 us
  transfers between devices with their start and end apart: 16, of which 8 were waited for; matrix products, arithmetic and copies ran while one was open for 6% of the time, Pallas kernels for 26%

profile of v2, /device:TPU:24, one launch (start us, length us, event | category | flops | bytes accessed | tf_op | source)
XLA Modules:
  0.0 213.8 jit_solution(14278765692351562394)
XLA Ops:
  7.3 9.8 %shard_map.82 = (f32[128,1024]{1,0:T(8,128)}, f32[128,1024]{1,0:T(8,128)}, bf16[128,120,128]{2,1,0:T(8,128)(2,1)}) custom-call(s32[8,1024]{1,0:T(8,128)} %bitcast.55, f32[8,1024]{1,0:T(8,128)} %bitcast.56, s32[1,128]{1,0:T(1,128)} %bitcast.57, bf16[224,1024]{1,0:T(8,128)(2,1)} %bitcast.52), custom_call_target="tpu_custom_call" | custom-call | flops 4831838208 | bytes 6000000 | tf_op jit(solution)/shard_map/pallas_call | solution.py:96
  17.1 63.0 %all_to_all.10 = bf16[128,120,128]{2,1,0:T(8,128)(2,1)} all-to-all(bf16[128,120,128]{2,1,0:T(8,128)(2,1)} %get-tuple-element.28), channel_id=1, replica_groups=mesh['dp'=8,'tp'=16] {'dp','tp'}, dimensions={0} | all-to-all | bytes 7864320 | tf_op jit(solution)/shard_map/all_to_all | solution.py:382
  80.1 23.1 %shard_map.83 = bf16[8,16,120,128]{3,2,1,0:T(8,128)(2,1)} custom-call(bf16[8,16,120,128]{3,2,1,0:T(8,128)(2,1)} %bitcast.50, bf16[3584,2048]{1,0:T(8,128)(2,1)} %bitcast.53, bf16[1024,3584]{1,0:T(8,128)(2,1)} %bitcast.54), custom_call_target="tpu_custom_call" | custom-call | flops 12683575296 | bytes 22020096 | tf_op jit(solution)/shard_map/pallas_call | solution.py:191
  103.2 6.6 %all-to-all-start.1 = ((bf16[128,120,128]{2,1,0:T(8,128)(2,1)}), bf16[128,120,128]{2,1,0:T(8,128)(2,1)}, u32[]{:S(2)}, u32[]{:S(2)}) async-start(bf16[128,120,128]{2,1,0:T(8,128)(2,1)} %bitcast.49), calls=%async_computation.1 | async-start | bytes 7864320 | tf_op jit(solution)/shard_map/all_to_all | solution.py:382
  110.3 1.6 gather_fusion.1
  111.9 1.6 gather_fusion
  113.5 10.6 %shard_map.84 = (bf16[1024,8192]{1,0:T(8,128)(2,1)}, bf16[1024,1024]{1,0:T(8,128)(2,1)}) custom-call(f32[128,1024]{1,0:T(8,128)} %get-tuple-element.30.rank_ref, f32[128,1024]{1,0:T(8,128)} %get-tuple-element.31.weight_ref), custom_call_target="tpu_custom_call" | custom-call | flops 16777216 | bytes 20000000 | tf_op jit(solution)/shard_map/pallas_call | solution.py:233
  124.0 1.7 copy_bitcast_fusion
  125.7 9.4 %all-gather.2.cloned.1.call-done = bf16[3584,1024]{1,0:T(8,128)(2,1)} async-done(((bf16[224,1024]{1,0:T(8,128)(2,1)}), bf16[3584,1024]{1,0:T(8,128)(2,1)}) %all-gather.2.cloned.1.call-update) | async-done | bytes 7340048 | tf_op jit(solution)/shard_map/all_gather | solution.py:376
  135.1 5.7 %fusion = f32[256,1024]{1,0:T(8,128)S(1)} fusion(bf16[3584,1024]{1,0:T(8,128)(2,1)} %all-gather.2.cloned.1.call-done, bf16[448,8,2,128]{3,2,1,0:T(2,128)(2,1)} %bitcast.48), kind=kOutput, calls=%fused_computation.2 | convolution fusion | flops 1879048192 | bytes 10223616 | tf_op jit(solution)/shard_map/dot_general | solution.py:27
  141.0 8.9 %collective-permute-start.5 = (bf16[128,512]{1,0:T(8,128)(2,1)S(1)}, bf16[128,512]{1,0:T(8,128)(2,1)S(1)}, u32[]{:S(2)}, u32[]{:S(2)}) collective-permute-start(bf16[128,512]{1,0:T(8,128)(2,1)S(1)} %get-tuple-element.49), channel_id=1, source_target_pairs={{8,0},{9,1},{10,2},{11,3},{12,4},{13,5},{14,6},{15,7},{0,8},{1,9},... | collective-permute-start | bytes 393224 | tf_op jit(solution)/shard_map/ppermute | solution.py:340
  150.0 2.0 collective-permute-start.3
  152.0 7.2 %collective-permute-start.2 = (bf16[128,512]{1,0:T(8,128)(2,1)S(1)}, bf16[128,512]{1,0:T(8,128)(2,1)S(1)}, u32[]{:S(2)}, u32[]{:S(2)}) collective-permute-start(bf16[128,512]{1,0:T(8,128)(2,1)S(1)} %get-tuple-element.50), channel_id=1, source_target_pairs={{2,0},{3,1},{0,2},{1,3},{6,4},{7,5},{4,6},{5,7},{10,8},{11,9},{8,1... | collective-permute-start | bytes 393224 | tf_op jit(solution)/shard_map/ppermute | solution.py:333
  160.0 2.8 %collective-permute-start = (bf16[128,512]{1,0:T(8,128)(2,1)S(1)}, bf16[128,512]{1,0:T(8,128)(2,1)S(1)}, u32[]{:S(2)}, u32[]{:S(2)}) collective-permute-start(bf16[128,512]{1,0:T(8,128)(2,1)S(1)} %get-tuple-element.50), channel_id=1, source_target_pairs={{1,0},{2,1},{3,2},{0,3},{5,4},{6,5},{7,6},{4,7},{9,8},{10,9},{11,1... | collective-permute-start | bytes 393224 | tf_op jit(solution)/shard_map/ppermute | solution.py:333
  162.9 2.5 %collective-permute-done.1 = bf16[128,512]{1,0:T(8,128)(2,1)S(1)} collective-permute-done((bf16[128,512]{1,0:T(8,128)(2,1)S(1)}, bf16[128,512]{1,0:T(8,128)(2,1)S(1)}, u32[]{:S(2)}, u32[]{:S(2)}) %collective-permute-start.1) | collective-permute-done | bytes 131104 | tf_op jit(solution)/shard_map/ppermute | solution.py:333
  166.0 1.8 collective-permute-start.9
  167.8 1.8 collective-permute-start.8
  169.6 0.9 pad_maximum_fusion.refs_0_
  170.5 2.0 collective-permute-start.7
  172.5 11.3 %shard_map.85.routed_ref = f32[224,1024]{1,0:T(8,128)} custom-call(bf16[128,120,128]{2,1,0:T(8,128)(2,1)} %all-to-all-done.1.back_ref, bf16[1024,8192]{1,0:T(8,128)(2,1)} %get-tuple-element.42.main_ref, bf16[1024,1024]{1,0:T(8,128)(2,1)} %get-tuple-element.43.late_ref), custom_call_target="tpu_custom_call" | custom-call | flops 4831838208 | bytes 24000000 | tf_op jit(solution)/shard_map/pallas_call | solution.py:285
  183.8 1.3 collective-permute-done.6.refs_1_
  185.1 1.0 slice.29
  186.1 1.0 slice.28
  187.0 1.0 slice.31
  188.0 1.0 slice.30
  189.1 3.2 %collective-permute-start.13 = (bf16[256,512]{1,0:T(8,128)(2,1)S(1)}, bf16[256,512]{1,0:T(8,128)(2,1)S(1)}, u32[]{:S(2)}, u32[]{:S(2)}) collective-permute-start(bf16[256,512]{1,0:T(8,128)(2,1)S(1)} %slice.31), channel_id=1, source_target_pairs={{1,0},{2,1},{3,2},{0,3},{5,4},{6,5},{7,6},{4,7},{9,8},{10,9},{11,1... | collective-permute-start | bytes 786440 | tf_op jit(solution)/shard_map/ppermute | solution.py:333
  192.3 1.9 collective-permute-start.10
  194.3 2.3 %collective-permute-done.12.refs_8_ = bf16[256,512]{1,0:T(8,128)(2,1)S(1)} collective-permute-done((bf16[256,512]{1,0:T(8,128)(2,1)S(1)}, bf16[256,512]{1,0:T(8,128)(2,1)S(1)}, u32[]{:S(2)}, u32[]{:S(2)}) %collective-permute-start.12) | collective-permute-done | bytes 262176 | tf_op jit(solution)/shard_map/ppermute | solution.py:333
  196.6 2.0 collective-permute-done.10.refs_3_
  198.7 3.2 %collective-permute-done.11.refs_4_ = bf16[256,512]{1,0:T(8,128)(2,1)S(1)} collective-permute-done((bf16[256,512]{1,0:T(8,128)(2,1)S(1)}, bf16[256,512]{1,0:T(8,128)(2,1)S(1)}, u32[]{:S(2)}, u32[]{:S(2)}) %collective-permute-start.11) | collective-permute-done | bytes 262176 | tf_op jit(solution)/shard_map/ppermute | solution.py:340
  201.8 1.2 copy-done.1
  203.0 4.0 %shard_map.86 = bf16[224,1024]{1,0:T(8,128)(2,1)} custom-call(bf16[224,2048]{1,0:T(8,128)(2,1)S(1)} %get-tuple-element.33.weights_a_ref, bf16[224,2048]{1,0:T(8,128)(2,1)S(1)} %get-tuple-element.34.weights_b_ref, f32[224,1024]{1,0:T(8,128)S(1)} %copy-done.1, bf16[512,512]{1,0:T(8,128)(2,1)} %pad_maximum_fusion.refs_0_, ...), custom_call_target="tpu_custom_call" | custom-call | flops 1000000000 | bytes 7000000 | tf_op jit(solution)/shard_map/pallas_call | solution.py:318
  (28 shorter events, 3.0 us)
Async XLA Ops:
  6.5 103.6 %copy-start = (bf16[2048,224]{0,1:T(8,128)(2,1)S(1)}, bf16[2048,224]{0,1:T(8,128)(2,1)}, u32[]{:S(2)}) copy-start(bf16[2048,224]{0,1:T(8,128)(2,1)} %param.15) | copy-start | bytes 2752516
  6.5 128.6 %all-gather.2.cloned.1.call-start = ((), (), s32[]{:S(2)}) async-start(), calls=%async_computation.2 | async-start | bytes 7798784 | tf_op jit(solution)/shard_map/all_gather | solution.py:376
  103.2 69.4 %all-to-all-start.1 = ((bf16[128,120,128]{2,1,0:T(8,128)(2,1)}), bf16[128,120,128]{2,1,0:T(8,128)(2,1)}, u32[]{:S(2)}, u32[]{:S(2)}) async-start(bf16[128,120,128]{2,1,0:T(8,128)(2,1)} %bitcast.49), calls=%async_computation.1 | async-start | bytes 7864320 | tf_op jit(solution)/shard_map/all_to_all | solution.py:382
  141.0 19.0 %collective-permute-start.5 = (bf16[128,512]{1,0:T(8,128)(2,1)S(1)}, bf16[128,512]{1,0:T(8,128)(2,1)S(1)}, u32[]{:S(2)}, u32[]{:S(2)}) collective-permute-start(bf16[128,512]{1,0:T(8,128)(2,1)S(1)} %get-tuple-element.49), channel_id=1, source_target_pairs={{8,0},{9,1},{10,2},{11,3},{12,4},{13,5},{14,6},{15,7},{0,8},{1,9},... | collective-permute-start | bytes 393224 | tf_op jit(solution)/shard_map/ppermute | solution.py:340
  149.9 13.0 %collective-permute-start.4 = (bf16[128,512]{1,0:T(8,128)(2,1)S(1)}, bf16[128,512]{1,0:T(8,128)(2,1)S(1)}, u32[]{:S(2)}, u32[]{:S(2)}) collective-permute-start(bf16[128,512]{1,0:T(8,128)(2,1)S(1)} %get-tuple-element.49), channel_id=1, source_target_pairs={{12,0},{13,1},{14,2},{15,3},{0,4},{1,5},{2,6},{3,7},{4,8},{5,9},{6... | collective-permute-start | bytes 393224 | tf_op jit(solution)/shard_map/ppermute | solution.py:340
  150.0 12.9 %collective-permute-start.3 = (bf16[128,512]{1,0:T(8,128)(2,1)S(1)}, bf16[128,512]{1,0:T(8,128)(2,1)S(1)}, u32[]{:S(2)}, u32[]{:S(2)}) collective-permute-start(bf16[128,512]{1,0:T(8,128)(2,1)S(1)} %get-tuple-element.49), channel_id=1, source_target_pairs={{4,0},{5,1},{6,2},{7,3},{8,4},{9,5},{10,6},{11,7},{12,8},{13,9},{1... | collective-permute-start | bytes 393224 | tf_op jit(solution)/shard_map/ppermute | solution.py:340
  152.0 10.9 %collective-permute-start.2 = (bf16[128,512]{1,0:T(8,128)(2,1)S(1)}, bf16[128,512]{1,0:T(8,128)(2,1)S(1)}, u32[]{:S(2)}, u32[]{:S(2)}) collective-permute-start(bf16[128,512]{1,0:T(8,128)(2,1)S(1)} %get-tuple-element.50), channel_id=1, source_target_pairs={{2,0},{3,1},{0,2},{1,3},{6,4},{7,5},{4,6},{5,7},{10,8},{11,9},{8,1... | collective-permute-start | bytes 393224 | tf_op jit(solution)/shard_map/ppermute | solution.py:333
  159.2 6.2 %collective-permute-start.1 = (bf16[128,512]{1,0:T(8,128)(2,1)S(1)}, bf16[128,512]{1,0:T(8,128)(2,1)S(1)}, u32[]{:S(2)}, u32[]{:S(2)}) collective-permute-start(bf16[128,512]{1,0:T(8,128)(2,1)S(1)} %get-tuple-element.50), channel_id=1, source_target_pairs={{3,0},{0,1},{1,2},{2,3},{7,4},{4,5},{5,6},{6,7},{11,8},{8,9},{9,10... | collective-permute-start | bytes 393224 | tf_op jit(solution)/shard_map/ppermute | solution.py:333
  160.0 5.9 %collective-permute-start = (bf16[128,512]{1,0:T(8,128)(2,1)S(1)}, bf16[128,512]{1,0:T(8,128)(2,1)S(1)}, u32[]{:S(2)}, u32[]{:S(2)}) collective-permute-start(bf16[128,512]{1,0:T(8,128)(2,1)S(1)} %get-tuple-element.50), channel_id=1, source_target_pairs={{1,0},{2,1},{3,2},{0,3},{5,4},{6,5},{7,6},{4,7},{9,8},{10,9},{11,1... | collective-permute-start | bytes 393224 | tf_op jit(solution)/shard_map/ppermute | solution.py:333
  166.0 17.8 %collective-permute-start.9 = (bf16[512,512]{1,0:T(8,128)(2,1)S(1)}, bf16[512,512]{1,0:T(8,128)(2,1)}, u32[]{:S(2)}, u32[]{:S(2)}) collective-permute-start(bf16[512,512]{1,0:T(8,128)(2,1)S(1)} %pad_maximum_fusion.1.refs_5_), channel_id=1, source_target_pairs={{3,0},{0,1},{1,2},{2,3},{7,4},{4,5},{5,6},{6,7},{11,8},{8,9},{9,10... | collective-permute-start | bytes 1572872 | tf_op jit(solution)/shard_map/ppermute | solution.py:333
  167.8 16.0 %collective-permute-start.8 = (bf16[512,512]{1,0:T(8,128)(2,1)S(1)}, bf16[512,512]{1,0:T(8,128)(2,1)}, u32[]{:S(2)}, u32[]{:S(2)}) collective-permute-start(bf16[512,512]{1,0:T(8,128)(2,1)S(1)} %pad_maximum_fusion.1.refs_5_), channel_id=1, source_target_pairs={{1,0},{2,1},{3,2},{0,3},{5,4},{6,5},{7,6},{4,7},{9,8},{10,9},{11,1... | collective-permute-start | bytes 1572872 | tf_op jit(solution)/shard_map/ppermute | solution.py:333
  170.5 13.3 %collective-permute-start.7 = (bf16[512,512]{1,0:T(8,128)(2,1)}, bf16[512,512]{1,0:T(8,128)(2,1)}, u32[]{:S(2)}, u32[]{:S(2)}) collective-permute-start(bf16[512,512]{1,0:T(8,128)(2,1)} %pad_maximum_fusion.refs_0_), channel_id=1, source_target_pairs={{12,0},{13,1},{14,2},{15,3},{0,4},{1,5},{2,6},{3,7},{4,8},{5,9},{6... | collective-permute-start | bytes 1572872 | tf_op jit(solution)/shard_map/ppermute | solution.py:340
  172.5 12.6 %collective-permute-start.6 = (bf16[512,512]{1,0:T(8,128)(2,1)}, bf16[512,512]{1,0:T(8,128)(2,1)}, u32[]{:S(2)}, u32[]{:S(2)}) collective-permute-start(bf16[512,512]{1,0:T(8,128)(2,1)} %pad_maximum_fusion.refs_0_), channel_id=1, source_target_pairs={{4,0},{5,1},{6,2},{7,3},{8,4},{9,5},{10,6},{11,7},{12,8},{13,9},{1... | collective-permute-start | bytes 1572872 | tf_op jit(solution)/shard_map/ppermute | solution.py:340
  189.0 7.7 %collective-permute-start.12 = (bf16[256,512]{1,0:T(8,128)(2,1)S(1)}, bf16[256,512]{1,0:T(8,128)(2,1)S(1)}, u32[]{:S(2)}, u32[]{:S(2)}) collective-permute-start(bf16[256,512]{1,0:T(8,128)(2,1)S(1)} %slice.30), channel_id=1, source_target_pairs={{3,0},{0,1},{1,2},{2,3},{7,4},{4,5},{5,6},{6,7},{11,8},{8,9},{9,10... | collective-permute-start | bytes 786440 | tf_op jit(solution)/shard_map/ppermute | solution.py:333
  189.1 7.6 %collective-permute-start.13 = (bf16[256,512]{1,0:T(8,128)(2,1)S(1)}, bf16[256,512]{1,0:T(8,128)(2,1)S(1)}, u32[]{:S(2)}, u32[]{:S(2)}) collective-permute-start(bf16[256,512]{1,0:T(8,128)(2,1)S(1)} %slice.31), channel_id=1, source_target_pairs={{1,0},{2,1},{3,2},{0,3},{5,4},{6,5},{7,6},{4,7},{9,8},{10,9},{11,1... | collective-permute-start | bytes 786440 | tf_op jit(solution)/shard_map/ppermute | solution.py:333
  192.3 6.4 %collective-permute-start.10 = (bf16[256,512]{1,0:T(8,128)(2,1)S(1)}, bf16[256,512]{1,0:T(8,128)(2,1)S(1)}, u32[]{:S(2)}, u32[]{:S(2)}) collective-permute-start(bf16[256,512]{1,0:T(8,128)(2,1)S(1)} %slice.28), channel_id=1, source_target_pairs={{12,0},{13,1},{14,2},{15,3},{0,4},{1,5},{2,6},{3,7},{4,8},{5,9},{6... | collective-permute-start | bytes 786440 | tf_op jit(solution)/shard_map/ppermute | solution.py:340
  194.2 7.6 %collective-permute-start.11 = (bf16[256,512]{1,0:T(8,128)(2,1)S(1)}, bf16[256,512]{1,0:T(8,128)(2,1)S(1)}, u32[]{:S(2)}, u32[]{:S(2)}) collective-permute-start(bf16[256,512]{1,0:T(8,128)(2,1)S(1)} %slice.29), channel_id=1, source_target_pairs={{4,0},{5,1},{6,2},{7,3},{8,4},{9,5},{10,6},{11,7},{12,8},{13,9},{1... | collective-permute-start | bytes 786440 | tf_op jit(solution)/shard_map/ppermute | solution.py:340
  201.8 1.2 copy-start.1
Sparse Core Ops, SparseCore 0:
  9.5 125.5 all-gather.1

commit v3 on v1

--- a/solution.py
+++ b/solution.py
@@ -285,8 +285,9 @@
     experts = back.shape[0]
     tokens = main.shape[0]
     last = earlier is not None
-    steps = experts // per_step // 2
-    base = steps if last else 0
+    blocks = experts // per_step
+    base = blocks // 4 if last else 0
+    steps = blocks - base if last else blocks // 4
     sums = pl.BlockSpec((tokens, 256), lambda i: (0, 0))
     out = pl.BlockSpec((feats, tokens), lambda i: (0, 0)) if last else sums
     return pl.pallas_call(
@@ -303,7 +304,7 @@
         scratch_shapes=[pltpu.VMEM((tokens, 256), F32)] * last,
         compiler_params=params(("arbitrary",), 56 * 1024 * 1024),
         cost_estimate=pl.CostEstimate(
-            flops=experts * 72 * 256 * tokens, bytes_accessed=12 * 10**6, transcendentals=0
+            flops=2 * steps * per_step * 72 * 256 * tokens, bytes_accessed=steps * 6 * 10**6, transcendentals=0
         ),
     )(back, main, late, *([earlier] if last else []))
 

time: 210 us -> 210 us (level)
  transfers between devices with their start and end apart: 16 -> 16, of which waited for: 8 -> 6; matrix products, arithmetic and copies ran while one was open for 5% -> 5% of each run, Pallas kernels for 28% -> 29%
where the time goes in v3:
time: 210 us; the launch traced here: 209 us
  blocking collectives  63 us (30%)
  Pallas kernels  61.6 us (29%)
  starting transfers between devices  38.7 us (18%)
  waiting for transfers between devices  20.9 us (10%)
  between operations  13.7 us (7%)
  matrix products  5.73 us (3%)
  local copies, waits for them, and re-layouts  5.37 us (3%)
    all_to_all x1, blocking collectives, exchange(): lax.all_to_all(blocks, ('dp', 'tp'), split_axis=0, concat_axis=0, tiled=T...  63 us
    pallas_call x1, Pallas kernels, expert(): pl.pallas_call(functools.partial(expert_kernel, tile), out_shape=jax.Shap...  23.1 us
    ppermute x7, starting transfers between devices, from_x(): return lax.ppermute(value, 'tp', pairs)  16.6 us
    pallas_call x2, Pallas kernels, combine(): pl.pallas_call(functools.partial(combine_kernel, last), out_shape=jax.Sha...  16.2 us
    ppermute x7, starting transfers between devices, from_y(): return lax.ppermute(value, 'tp', pairs)  15.4 us
    pallas_call x1, Pallas kernels, spread(): pl.pallas_call(spread_kernel, out_shape=(jax.ShapeDtypeStruct((tokens, ex...  10.6 us
    all_gather x1, waiting for transfers between devices, on_device(): features_all = lax.all_gather(features, 'tp', axis=0, tiled=True)  10.4 us
    pallas_call x1, Pallas kernels, dispatch(): pl.pallas_call(functools.partial(dispatch_kernel, per_step), out_shape=(t...  9.8 us
  transfers between devices with their start and end apart: 16, of which 6 were waited for; matrix products, arithmetic and copies ran while one was open for 5% of the time, Pallas kernels for 29%

profile of v3, /device:TPU:24, one launch (start us, length us, event | category | flops | bytes accessed | tf_op | source)
XLA Modules:
  0.0 209.2 jit_solution(15142448950051546985)
XLA Ops:
  6.5 0.7 all-gather.2.cloned.1.call-update
  7.3 9.8 %shard_map.82 = (f32[128,1024]{1,0:T(8,128)}, f32[128,1024]{1,0:T(8,128)}, bf16[128,120,128]{2,1,0:T(8,128)(2,1)}) custom-call(s32[8,1024]{1,0:T(8,128)} %bitcast.55, f32[8,1024]{1,0:T(8,128)} %bitcast.56, s32[1,128]{1,0:T(1,128)} %bitcast.57, bf16[224,1024]{1,0:T(8,128)(2,1)} %bitcast.52), custom_call_target="tpu_custom_call" | custom-call | flops 4831838208 | bytes 6000000 | tf_op jit(solution)/shard_map/pallas_call | solution.py:96
  17.1 63.0 %all_to_all.10 = bf16[128,120,128]{2,1,0:T(8,128)(2,1)} all-to-all(bf16[128,120,128]{2,1,0:T(8,128)(2,1)} %get-tuple-element.28), channel_id=1, replica_groups=mesh['dp'=8,'tp'=16] {'dp','tp'}, dimensions={0} | all-to-all | bytes 7864320 | tf_op jit(solution)/shard_map/all_to_all | solution.py:387
  80.0 23.1 %shard_map.83 = bf16[8,16,120,128]{3,2,1,0:T(8,128)(2,1)} custom-call(bf16[8,16,120,128]{3,2,1,0:T(8,128)(2,1)} %bitcast.50, bf16[3584,2048]{1,0:T(8,128)(2,1)} %bitcast.53, bf16[1024,3584]{1,0:T(8,128)(2,1)} %bitcast.54), custom_call_target="tpu_custom_call" | custom-call | flops 12683575296 | bytes 22020096 | tf_op jit(solution)/shard_map/pallas_call | solution.py:191
  103.1 6.6 %all-to-all-start.1 = ((bf16[128,120,128]{2,1,0:T(8,128)(2,1)}), bf16[128,120,128]{2,1,0:T(8,128)(2,1)}, u32[]{:S(2)}, u32[]{:S(2)}) async-start(bf16[128,120,128]{2,1,0:T(8,128)(2,1)} %bitcast.49), calls=%async_computation.1 | async-start | bytes 7864320 | tf_op jit(solution)/shard_map/all_to_all | solution.py:387
  110.1 0.2 copy_bitcast_fusion.2
  110.3 0.7 gather_fusion.1
  111.0 1.6 gather_fusion
  112.6 10.6 %shard_map.84 = (bf16[1024,8192]{1,0:T(8,128)(2,1)}, bf16[1024,1024]{1,0:T(8,128)(2,1)}) custom-call(f32[128,1024]{1,0:T(8,128)} %get-tuple-element.30.rank_ref, f32[128,1024]{1,0:T(8,128)} %get-tuple-element.31.weight_ref), custom_call_target="tpu_custom_call" | custom-call | flops 16777216 | bytes 20000000 | tf_op jit(solution)/shard_map/pallas_call | solution.py:233
  123.2 1.4 copy_bitcast_fusion
  124.6 10.4 %all-gather.2.cloned.1.call-done = bf16[3584,1024]{1,0:T(8,128)(2,1)} async-done(((bf16[224,1024]{1,0:T(8,128)(2,1)}), bf16[3584,1024]{1,0:T(8,128)(2,1)}) %all-gather.2.cloned.1.call-update) | async-done | bytes 7340048 | tf_op jit(solution)/shard_map/all_gather | solution.py:381
  135.1 5.7 %fusion = f32[256,1024]{1,0:T(8,128)S(1)} fusion(bf16[3584,1024]{1,0:T(8,128)(2,1)} %all-gather.2.cloned.1.call-done, bf16[448,8,2,128]{3,2,1,0:T(2,128)(2,1)} %bitcast.48), kind=kOutput, calls=%fused_computation.2 | convolution fusion | flops 1879048192 | bytes 10223616 | tf_op jit(solution)/shard_map/dot_general | solution.py:27
  140.8 0.2 fusion.3
  141.0 8.9 %collective-permute-start.5 = (bf16[128,512]{1,0:T(8,128)(2,1)S(1)}, bf16[128,512]{1,0:T(8,128)(2,1)S(1)}, u32[]{:S(2)}, u32[]{:S(2)}) collective-permute-start(bf16[128,512]{1,0:T(8,128)(2,1)S(1)} %get-tuple-element.49), channel_id=1, source_target_pairs={{8,0},{9,1},{10,2},{11,3},{12,4},{13,5},{14,6},{15,7},{0,8},{1,9},... | collective-permute-start | bytes 393224 | tf_op jit(solution)/shard_map/ppermute | solution.py:344
  149.9 0.2 collective-permute-start.4
  150.1 1.9 collective-permute-start.3
  151.9 7.2 %collective-permute-start.2 = (bf16[128,512]{1,0:T(8,128)(2,1)S(1)}, bf16[128,512]{1,0:T(8,128)(2,1)S(1)}, u32[]{:S(2)}, u32[]{:S(2)}) collective-permute-start(bf16[128,512]{1,0:T(8,128)(2,1)S(1)} %get-tuple-element.50), channel_id=1, source_target_pairs={{2,0},{3,1},{0,2},{1,3},{6,4},{7,5},{4,6},{5,7},{10,8},{11,9},{8,1... | collective-permute-start | bytes 393224 | tf_op jit(solution)/shard_map/ppermute | solution.py:337
  159.1 0.9 collective-permute-done.5
  160.0 2.8 %collective-permute-start = (bf16[128,512]{1,0:T(8,128)(2,1)S(1)}, bf16[128,512]{1,0:T(8,128)(2,1)S(1)}, u32[]{:S(2)}, u32[]{:S(2)}) collective-permute-start(bf16[128,512]{1,0:T(8,128)(2,1)S(1)} %get-tuple-element.50), channel_id=1, source_target_pairs={{1,0},{2,1},{3,2},{0,3},{5,4},{6,5},{7,6},{4,7},{9,8},{10,9},{11,1... | collective-permute-start | bytes 393224 | tf_op jit(solution)/shard_map/ppermute | solution.py:337
  162.9 5.1 %shard_map.85.refs_0_ = f32[1024,256]{1,0:T(8,128)} custom-call(bf16[128,120,128]{2,1,0:T(8,128)(2,1)} %all-to-all-done.1.back_ref, bf16[1024,8192]{1,0:T(8,128)(2,1)} %get-tuple-element.36.main_ref, bf16[1024,1024]{1,0:T(8,128)(2,1)} %get-tuple-element.32.late_ref), custom_call_target="tpu_custom_call" | custom-call | flops 1207959552 | bytes 6000000 | tf_op jit(solution)/shard_map/pallas_call | solution.py:293
  168.1 3.2 %collective-permute-start.8 = (bf16[512,512]{1,0:T(8,128)(2,1)S(1)}, bf16[512,512]{1,0:T(8,128)(2,1)S(1)}, u32[]{:S(2)}, u32[]{:S(2)}) collective-permute-start(bf16[512,512]{1,0:T(8,128)(2,1)S(1)} %pad_maximum_fusion.1.refs_5_), channel_id=1, source_target_pairs={{1,0},{2,1},{3,2},{0,3},{5,4},{6,5},{7,6},{4,7},{9,8},{10,9},{11,1... | collective-permute-start | bytes 1572872 | tf_op jit(solution)/shard_map/ppermute | solution.py:337
  171.4 2.4 %collective-permute-start.7 = (bf16[512,512]{1,0:T(8,128)(2,1)S(1)}, bf16[512,512]{1,0:T(8,128)(2,1)S(1)}, u32[]{:S(2)}, u32[]{:S(2)}) collective-permute-start(bf16[512,512]{1,0:T(8,128)(2,1)S(1)} %pad_maximum_fusion.refs_0_), channel_id=1, source_target_pairs={{12,0},{13,1},{14,2},{15,3},{0,4},{1,5},{2,6},{3,7},{4,8},{5,9},{6... | collective-permute-start | bytes 1572872 | tf_op jit(solution)/shard_map/ppermute | solution.py:344
  173.8 11.2 %shard_map.86.routed_ref = f32[224,1024]{1,0:T(8,128)} custom-call(bf16[128,120,128]{2,1,0:T(8,128)(2,1)} %all-to-all-done.1.back_ref, bf16[1024,8192]{1,0:T(8,128)(2,1)} %get-tuple-element.36.main_ref, bf16[1024,1024]{1,0:T(8,128)(2,1)} %get-tuple-element.32.late_ref, f32[1024,256]{1,0:T(8,128)} %shard_map.85.refs_0_), custom_call_target="tpu_custom_call" | custom-call | flops 3623878656 | bytes 18000000 | tf_op jit(solution)/shard_map/pallas_call | solution.py:293
  185.0 1.7 collective-permute-done.6.refs_1_
  186.9 3.2 %collective-permute-start.13 = (bf16[256,512]{1,0:T(8,128)(2,1)S(1)}, bf16[256,512]{1,0:T(8,128)(2,1)S(1)}, u32[]{:S(2)}, u32[]{:S(2)}) collective-permute-start(bf16[256,512]{1,0:T(8,128)(2,1)S(1)} %slice.31), channel_id=1, source_target_pairs={{1,0},{2,1},{3,2},{0,3},{5,4},{6,5},{7,6},{4,7},{9,8},{10,9},{11,1... | collective-permute-start | bytes 786440 | tf_op jit(solution)/shard_map/ppermute | solution.py:337
  190.1 1.6 collective-permute-start.10
  191.7 0.4 collective-permute-start.11
  192.1 2.3 %collective-permute-done.12.refs_8_ = bf16[256,512]{1,0:T(8,128)(2,1)S(1)} collective-permute-done((bf16[256,512]{1,0:T(8,128)(2,1)S(1)}, bf16[256,512]{1,0:T(8,128)(2,1)S(1)}, u32[]{:S(2)}, u32[]{:S(2)}) %collective-permute-start.12) | collective-permute-done | bytes 262176 | tf_op jit(solution)/shard_map/ppermute | solution.py:337
  194.4 2.0 collective-permute-done.10.refs_3_
  196.5 2.8 %collective-permute-done.11.refs_4_ = bf16[256,512]{1,0:T(8,128)(2,1)S(1)} collective-permute-done((bf16[256,512]{1,0:T(8,128)(2,1)S(1)}, bf16[256,512]{1,0:T(8,128)(2,1)S(1)}, u32[]{:S(2)}, u32[]{:S(2)}) %collective-permute-start.11) | collective-permute-done | bytes 262176 | tf_op jit(solution)/shard_map/ppermute | solution.py:344
  199.3 1.2 copy-done.2
  200.4 1.9 shard_map.87
  (31 shorter events, 0.6 us)
Async XLA Ops:
  6.5 103.6 %copy-start = (bf16[2048,224]{0,1:T(8,128)(2,1)S(1)}, bf16[2048,224]{0,1:T(8,128)(2,1)}, u32[]{:S(2)}) copy-start(bf16[2048,224]{0,1:T(8,128)(2,1)} %param.15) | copy-start | bytes 2752516
  6.5 128.5 %all-gather.2.cloned.1.call-start = ((), (), s32[]{:S(2)}) async-start(), calls=%async_computation.2 | async-start | bytes 7798784 | tf_op jit(solution)/shard_map/all_gather | solution.py:381
  103.1 59.8 %all-to-all-start.1 = ((bf16[128,120,128]{2,1,0:T(8,128)(2,1)}), bf16[128,120,128]{2,1,0:T(8,128)(2,1)}, u32[]{:S(2)}, u32[]{:S(2)}) async-start(bf16[128,120,128]{2,1,0:T(8,128)(2,1)} %bitcast.49), calls=%async_computation.1 | async-start | bytes 7864320 | tf_op jit(solution)/shard_map/all_to_all | solution.py:387
  141.0 19.1 %collective-permute-start.5 = (bf16[128,512]{1,0:T(8,128)(2,1)S(1)}, bf16[128,512]{1,0:T(8,128)(2,1)S(1)}, u32[]{:S(2)}, u32[]{:S(2)}) collective-permute-start(bf16[128,512]{1,0:T(8,128)(2,1)S(1)} %get-tuple-element.49), channel_id=1, source_target_pairs={{8,0},{9,1},{10,2},{11,3},{12,4},{13,5},{14,6},{15,7},{0,8},{1,9},... | collective-permute-start | bytes 393224 | tf_op jit(solution)/shard_map/ppermute | solution.py:344
  149.9 18.0 %collective-permute-start.4 = (bf16[128,512]{1,0:T(8,128)(2,1)S(1)}, bf16[128,512]{1,0:T(8,128)(2,1)S(1)}, u32[]{:S(2)}, u32[]{:S(2)}) collective-permute-start(bf16[128,512]{1,0:T(8,128)(2,1)S(1)} %get-tuple-element.49), channel_id=1, source_target_pairs={{12,0},{13,1},{14,2},{15,3},{0,4},{1,5},{2,6},{3,7},{4,8},{5,9},{6... | collective-permute-start | bytes 393224 | tf_op jit(solution)/shard_map/ppermute | solution.py:344
  150.1 17.9 %collective-permute-start.3 = (bf16[128,512]{1,0:T(8,128)(2,1)S(1)}, bf16[128,512]{1,0:T(8,128)(2,1)S(1)}, u32[]{:S(2)}, u32[]{:S(2)}) collective-permute-start(bf16[128,512]{1,0:T(8,128)(2,1)S(1)} %get-tuple-element.49), channel_id=1, source_target_pairs={{4,0},{5,1},{6,2},{7,3},{8,4},{9,5},{10,6},{11,7},{12,8},{13,9},{1... | collective-permute-start | bytes 393224 | tf_op jit(solution)/shard_map/ppermute | solution.py:344
  151.9 16.0 %collective-permute-start.2 = (bf16[128,512]{1,0:T(8,128)(2,1)S(1)}, bf16[128,512]{1,0:T(8,128)(2,1)S(1)}, u32[]{:S(2)}, u32[]{:S(2)}) collective-permute-start(bf16[128,512]{1,0:T(8,128)(2,1)S(1)} %get-tuple-element.50), channel_id=1, source_target_pairs={{2,0},{3,1},{0,2},{1,3},{6,4},{7,5},{4,6},{5,7},{10,8},{11,9},{8,1... | collective-permute-start | bytes 393224 | tf_op jit(solution)/shard_map/ppermute | solution.py:337
  159.1 8.8 %collective-permute-start.1 = (bf16[128,512]{1,0:T(8,128)(2,1)S(1)}, bf16[128,512]{1,0:T(8,128)(2,1)S(1)}, u32[]{:S(2)}, u32[]{:S(2)}) collective-permute-start(bf16[128,512]{1,0:T(8,128)(2,1)S(1)} %get-tuple-element.50), channel_id=1, source_target_pairs={{3,0},{0,1},{1,2},{2,3},{7,4},{4,5},{5,6},{6,7},{11,8},{8,9},{9,10... | collective-permute-start | bytes 393224 | tf_op jit(solution)/shard_map/ppermute | solution.py:337
  160.0 7.9 %collective-permute-start = (bf16[128,512]{1,0:T(8,128)(2,1)S(1)}, bf16[128,512]{1,0:T(8,128)(2,1)S(1)}, u32[]{:S(2)}, u32[]{:S(2)}) collective-permute-start(bf16[128,512]{1,0:T(8,128)(2,1)S(1)} %get-tuple-element.50), channel_id=1, source_target_pairs={{1,0},{2,1},{3,2},{0,3},{5,4},{6,5},{7,6},{4,7},{9,8},{10,9},{11,1... | collective-permute-start | bytes 393224 | tf_op jit(solution)/shard_map/ppermute | solution.py:337
  168.0 17.0 %collective-permute-start.9 = (bf16[512,512]{1,0:T(8,128)(2,1)S(1)}, bf16[512,512]{1,0:T(8,128)(2,1)S(1)}, u32[]{:S(2)}, u32[]{:S(2)}) collective-permute-start(bf16[512,512]{1,0:T(8,128)(2,1)S(1)} %pad_maximum_fusion.1.refs_5_), channel_id=1, source_target_pairs={{3,0},{0,1},{1,2},{2,3},{7,4},{4,5},{5,6},{6,7},{11,8},{8,9},{9,10... | collective-permute-start | bytes 1572872 | tf_op jit(solution)/shard_map/ppermute | solution.py:337
  168.1 16.9 %collective-permute-start.8 = (bf16[512,512]{1,0:T(8,128)(2,1)S(1)}, bf16[512,512]{1,0:T(8,128)(2,1)S(1)}, u32[]{:S(2)}, u32[]{:S(2)}) collective-permute-start(bf16[512,512]{1,0:T(8,128)(2,1)S(1)} %pad_maximum_fusion.1.refs_5_), channel_id=1, source_target_pairs={{1,0},{2,1},{3,2},{0,3},{5,4},{6,5},{7,6},{4,7},{9,8},{10,9},{11,1... | collective-permute-start | bytes 1572872 | tf_op jit(solution)/shard_map/ppermute | solution.py:337
  171.4 13.6 %collective-permute-start.7 = (bf16[512,512]{1,0:T(8,128)(2,1)S(1)}, bf16[512,512]{1,0:T(8,128)(2,1)S(1)}, u32[]{:S(2)}, u32[]{:S(2)}) collective-permute-start(bf16[512,512]{1,0:T(8,128)(2,1)S(1)} %pad_maximum_fusion.refs_0_), channel_id=1, source_target_pairs={{12,0},{13,1},{14,2},{15,3},{0,4},{1,5},{2,6},{3,7},{4,8},{5,9},{6... | collective-permute-start | bytes 1572872 | tf_op jit(solution)/shard_map/ppermute | solution.py:344
  173.8 12.9 %collective-permute-start.6 = (bf16[512,512]{1,0:T(8,128)(2,1)S(1)}, bf16[512,512]{1,0:T(8,128)(2,1)S(1)}, u32[]{:S(2)}, u32[]{:S(2)}) collective-permute-start(bf16[512,512]{1,0:T(8,128)(2,1)S(1)} %pad_maximum_fusion.refs_0_), channel_id=1, source_target_pairs={{4,0},{5,1},{6,2},{7,3},{8,4},{9,5},{10,6},{11,7},{12,8},{13,9},{1... | collective-permute-start | bytes 1572872 | tf_op jit(solution)/shard_map/ppermute | solution.py:344
  186.7 15.6 %copy-start.1 = (bf16[2048,224]{0,1:T(8,128)(2,1)S(1)}, bf16[2048,224]{0,1:T(8,128)(2,1)}, u32[]{:S(2)}) copy-start(bf16[2048,224]{0,1:T(8,128)(2,1)} %param.15) | copy-start | bytes 2752516
  186.8 7.7 %collective-permute-start.12 = (bf16[256,512]{1,0:T(8,128)(2,1)S(1)}, bf16[256,512]{1,0:T(8,128)(2,1)S(1)}, u32[]{:S(2)}, u32[]{:S(2)}) collective-permute-start(bf16[256,512]{1,0:T(8,128)(2,1)S(1)} %slice.30), channel_id=1, source_target_pairs={{3,0},{0,1},{1,2},{2,3},{7,4},{4,5},{5,6},{6,7},{11,8},{8,9},{9,10... | collective-permute-start | bytes 786440 | tf_op jit(solution)/shard_map/ppermute | solution.py:337
  186.9 7.6 %collective-permute-start.13 = (bf16[256,512]{1,0:T(8,128)(2,1)S(1)}, bf16[256,512]{1,0:T(8,128)(2,1)S(1)}, u32[]{:S(2)}, u32[]{:S(2)}) collective-permute-start(bf16[256,512]{1,0:T(8,128)(2,1)S(1)} %slice.31), channel_id=1, source_target_pairs={{1,0},{2,1},{3,2},{0,3},{5,4},{6,5},{7,6},{4,7},{9,8},{10,9},{11,1... | collective-permute-start | bytes 786440 | tf_op jit(solution)/shard_map/ppermute | solution.py:337
  190.1 6.4 %collective-permute-start.10 = (bf16[256,512]{1,0:T(8,128)(2,1)S(1)}, bf16[256,512]{1,0:T(8,128)(2,1)S(1)}, u32[]{:S(2)}, u32[]{:S(2)}) collective-permute-start(bf16[256,512]{1,0:T(8,128)(2,1)S(1)} %slice.28), channel_id=1, source_target_pairs={{12,0},{13,1},{14,2},{15,3},{0,4},{1,5},{2,6},{3,7},{4,8},{5,9},{6... | collective-permute-start | bytes 786440 | tf_op jit(solution)/shard_map/ppermute | solution.py:344
  191.7 7.6 %collective-permute-start.11 = (bf16[256,512]{1,0:T(8,128)(2,1)S(1)}, bf16[256,512]{1,0:T(8,128)(2,1)S(1)}, u32[]{:S(2)}, u32[]{:S(2)}) collective-permute-start(bf16[256,512]{1,0:T(8,128)(2,1)S(1)} %slice.29), channel_id=1, source_target_pairs={{4,0},{5,1},{6,2},{7,3},{8,4},{9,5},{10,6},{11,7},{12,8},{13,9},{1... | collective-permute-start | bytes 786440 | tf_op jit(solution)/shard_map/ppermute | solution.py:344
  199.3 1.2 copy-start.2
Sparse Core Ops, SparseCore 0:
  9.5 125.5 all-gather.1
